TPU v7x, 32 devices: a whole 2x2x4 slice. The times are simulated.
32 devices in a mesh: batch: 4 (over x, core), ctx: 4 (over z), fsdp: 2 (over y).
Axes of the slice: x: 2, y: 2, z: 4, core: 2. Of those that a mesh axis runs over, the one named last changes fastest.
Arguments:
- layer_input: bfloat16 [8, 512, 1024], P(('batch', 'fsdp'), 'ctx'), may hold values from -6 to 6
- out_grad: bfloat16 [8, 512, 1024], P(('batch', 'fsdp'), 'ctx'), may hold values from -6 to 6
- span_order: int32 [4], replicated, may hold values from 0 to 3, each once
- inward: bfloat16 [1024, 3072], P('fsdp')
- inward_bias: bfloat16 [3072], P('fsdp'), may hold values from -3 to 3
- outward: bfloat16 [1024, 1024], P('fsdp'), may hold values from -1 to 1
- outward_bias: bfloat16 [1024], P('fsdp'), may hold values from -3 to 3
- expand: bfloat16 [1024, 4096], P('fsdp'), may hold values from -0.1875 to 0.1875
- expand_bias: bfloat16 [4096], P('fsdp'), may hold values from -3 to 3
- contract: bfloat16 [4096, 1024], P('fsdp'), may hold values from -0.09375 to 0.09375
- contract_bias: bfloat16 [1024], P('fsdp'), may hold values from -3 to 3
- first_gain: bfloat16 [1024], P('fsdp'), may hold values from 0.099609375 to 1.8984375
- first_bias: bfloat16 [1024], P('fsdp'), may hold values from -3 to 3
- second_gain: bfloat16 [1024], P('fsdp'), may hold values from 0.099609375 to 1.8984375
- second_bias: bfloat16 [1024], P('fsdp'), may hold values from -3 to 3
Outputs:
- output: bfloat16 [8, 512, 1024], P(('batch', 'fsdp'), 'ctx')
- input_grad: float32 [8, 512, 1024], P(('batch', 'fsdp'), 'ctx')
- inward_grad: float32 [1024, 3072], P('fsdp')
- inward_shift: float32 [3072], P('fsdp')
- outward_grad: float32 [1024, 1024], P('fsdp')
- outward_shift: float32 [1024], P('fsdp')
- expand_grad: float32 [1024, 4096], P('fsdp')
- expand_shift: float32 [4096], P('fsdp')
- contract_grad: float32 [4096, 1024], P('fsdp')
- contract_shift: float32 [1024], P('fsdp')
- first_scale: float32 [1024], P('fsdp')
- first_shift: float32 [1024], P('fsdp')
- second_scale: float32 [1024], P('fsdp')
- second_shift: float32 [1024], P('fsdp')
Inputs may be any that keep to these rules, and one draw needn't show every extreme that they name: `span_order`: each value appears once.
All inputs are finite; a program needn't handle non-finite values.
Results may differ from a plain program's by a relative error of at most 0.012.
The roundings to bfloat16 on the way count: a program that leaves them out, or rounds other values in their place, can miss the bound.
Values may be sent and summed in bfloat16 or wider, within the bound.
A program may use at most 320 MiB of HBM per device.

v0:
```python
import functools
import math

import jax
import jax.numpy as jnp
from jax import lax
from jax.experimental import pallas as pl
from jax.experimental.pallas import tpu as pltpu
from jax.sharding import PartitionSpec as P

HEAD_DIM = 64
ROT = 16

EPSILON = 1e-05
ROTARY_BASE = 10000.0
MASKED = -1e30
HALF_ROOT = 0.7071067811865476
NORMAL_PEAK = 0.3989422804014327
PLANE = ("batch", "fsdp")


MESH = pl.DeviceIdType.MESH
CORES = 2
VMEM_LIMIT = 56 * 2**20


def here():
    return (lax.axis_index("batch"), lax.axis_index("ctx"), lax.axis_index("fsdp"))


def swapped(index, step):
    return index + step * (1 - 2 * (index // step % 2))


def greet(partners):
    barrier = pltpu.get_barrier_semaphore()
    for partner in partners:
        pl.semaphore_signal(barrier, inc=1, device_id=partner, device_id_type=MESH)
    pl.semaphore_wait(barrier, len(partners))


def remote(src, dst, send, recv, target):
    return pltpu.make_async_remote_copy(
        src_ref=src,
        dst_ref=dst,
        send_sem=send,
        recv_sem=recv,
        device_id=target,
        device_id_type=MESH,
    )


def back_kernel(
    sizes,
    tokens,
    heads,
    counts,
    piece,
    part_in,
    mixed_in,
    out_in,
    second_in,
    first_rows_in,
    grads_in,
    inputs_in,
    mean_ref,
    inverse_ref,
    inward_in,
    outward_in,
    place_col,
    place_row,
    cosine_ref,
    fore_ref,
    aft_ref,
    vector_ref,
    sums_ref,
    token_ref,
    vector_out,
    part,
    mixed,
    out_rows,
    second_rows,
    first_back,
    first_rows,
    grads,
    inputs,
    inward,
    outward,
    attended,
    heads_sum,
    back_out,
    back_in,
    inward_sum,
    final,
    reduced,
    near,
    across_in,
    far,
    token_sum,
    vector_in,
    vector_sum,
    load_sems,
    store_sems,
    own_sems,
    turn_sems,
    reduce_sems,
    back_sems,
    row_sems,
    chip_sems,
    core_sems,
    near_sems,
    across_sems,
    far_sems,
    vector_sems,
):
    batch_count, context_count, fsdp_count = sizes
    early_other, early, late_other, late = counts
    b, z, y = here()
    chips = batch_count // CORES
    core = b % CORES
    chip = b // CORES
    width = part.shape[1]
    cols = heads * HEAD_DIM
    plane = batch_count * fsdp_count
    own_sequences = plane // context_count
    length = tokens * context_count
    steps = early + late
    early_rows = 2 * early * piece
    last = context_count - 1
    f32, half_type = (jnp.float32, part.dtype)

    sibling = (chip * CORES + (1 - core), z, y)
    across = (b, z, 1 - y)
    peers = [((chip + d) % chips * CORES + core, z, y) for d in range(1, chips)]
    sources = [(chip + chips - d) % chips * CORES + core for d in range(1, chips)]
    others = [(b, (z + d) % context_count, y) for d in range(1, context_count)]
    stages = []
    step = 1
    while step < batch_count:
        stages.append((swapped(b, step), z, y))
        step *= 2
    stages.append(across)
    step = 1
    while step < context_count:
        stages.append((b, swapped(z, step), y))
        step *= 2

    loads = [
        pltpu.make_async_copy(source, target, load_sems.at[i])
        for i, (source, target) in enumerate(
            [
                (part_in, part.at[pl.ds(0, early_rows), :]),
                (mixed_in, mixed),
                (second_in, second_rows),
                (out_in, out_rows),
                (first_rows_in, first_rows),
                (grads_in, grads),
                (inputs_in, inputs),
                (inward_in, inward),
                (outward_in, outward),
            ]
        )
    ]
    for load in loads:
        load.start()
    greet([sibling, across] + peers + others)

    def sem(sems, *index):
        return (sems.at[(0, *index)], sems.at[(1, *index)])


    def place(half, k):
        is_late = jnp.minimum(k // early, 1)
        other = early_other * (1 - is_late) + late_other * is_late
        count = early * (1 - is_late) + late * is_late
        j = k - early * is_late
        is_own = jnp.minimum(j // other, 1)
        row = (half * other + j) * (1 - is_own) + (
            2 * other + half * (count - other) + j - other
        ) * is_own
        return pl.multiple_of((2 * early * is_late + row) * piece, piece)

    def own(k):
        is_late = jnp.minimum(k // early, 1)
        other = early_other * (1 - is_late) + late_other * is_late
        return jnp.minimum((k - early * is_late) // other, 1)

    def rows_at(ref, row):
        return ref.at[pl.ds(row, piece), :]

    def final_at(slot, row):
        return final.at[slot, pl.ds(row, piece), :]

    def slot_of(k):
        return batch_count * (1 - own(k)) + b * own(k)

    def back_copy(half, k, target):
        at = final_at(slot_of(k), place(half, k))
        return remote(at, at, *sem(back_sems, half, k), target)

    def row_copy(half, k):
        row = place(half, k)
        source = final_at(batch_count, row)
        return remote(source, final_at(b, row), *sem(row_sems, half, k), across)

    def chip_copy(d, half, k, slot):
        at = final_at(slot, place(half, k))
        return remote(at, at, *sem(chip_sems, d, half, k), peers[d])

    def core_copy(d, half, k, slot):
        at = final_at(slot, place(half, k))
        return remote(at, at, *sem(core_sems, d, half, k), sibling)

    def spread(half, k):
        for d in range(chips - 1):
            chip_copy(d, half, k, b).start()
        core_copy(0, half, k, b).start()

    def finish(half, k, position, behind):
        @pl.when(position > 0)
        def _():
            back_copy(half, k, behind).start()

        @pl.when(own(k) == 0)
        def _():
            row_copy(half, k).start()

        @pl.when(own(k) == 1)
        def _():
            spread(half, k)

    def arrived(half, k):
        for d in range(chips - 1):
            chip_copy(d, half, k, sources[d]).wait_recv()
            core_copy(1 + d, half, k, sources[d]).start()

    def pieces(t, half):
        position = z if half == 0 else last - z
        ahead = (b, (z + 1 if half == 0 else z + last) % context_count, y)
        behind = (b, (z + last if half == 0 else z + 1) % context_count, y)
        k = t - position

        @pl.when((k >= 0) & (k < steps))
        def _():
            row = place(half, k)
            to_next = remote(
                rows_at(reduced, row), rows_at(reduced, row), *sem(reduce_sems, half, k), ahead
            )

            @pl.when(position == 0)
            def _():
                remote(
                    rows_at(part, row), rows_at(reduced, row), *sem(reduce_sems, half, k), ahead
                ).start()

            @pl.when(position > 0)
            def _():
                to_next.wait_recv()
                mine = part[pl.ds(row, piece), :].astype(f32)
                came = reduced[pl.ds(row, piece), :].astype(f32)
                summed = (mine + came).astype(half_type)

                @pl.when(position < last)
                def _():
                    reduced[pl.ds(row, piece), :] = summed
                    to_next.start()

                @pl.when(position == last)
                def _():
                    final[slot_of(k), pl.ds(row, piece), :] = summed
                    finish(half, k, position, behind)

        k_back = t - 2 * last + position

        @pl.when((position < last) & (k_back >= 0) & (k_back < steps))
        def _():
            back_copy(half, k_back, behind).wait_recv()
            finish(half, k_back, position, behind)

        k_row = k_back - 1

        @pl.when((k_row >= 0) & (k_row < steps))
        def _():
            @pl.when(own(k_row) == 0)
            def _():
                row_copy(half, k_row).wait_recv()
                spread(half, k_row)

            @pl.when(own(k_row) == 1)
            def _():
                arrived(half, k_row)

        k_chip = k_row - 2

        @pl.when((k_chip >= 0) & (k_chip < steps))
        def _():
            @pl.when(own(k_chip) == 0)
            def _():
                arrived(half, k_chip)


    def attend(n):
        s, h = (n // heads, n % heads)
        columns = [mixed[s, :, i * cols : (i + 1) * cols] for i in range(4)]
        lane = lax.broadcasted_iota(jnp.int32, (length, cols), 1) // HEAD_DIM
        picked = lane == h
        nothing = jnp.zeros((length, cols), half_type)
        queries, keys, values, upstream = columns
        queries_h, keys_h, values_h, upstream_h = [
            jnp.where(picked, column, nothing) for column in columns
        ]
        scale = 1.0 / math.sqrt(HEAD_DIM)
        scores = dot(queries_h, keys, ((1,), (1,))) * scale
        scores = jnp.where(place_row[...] <= place_col[...], scores, MASKED)
        peak = jnp.max(scores, axis=1, keepdims=True)
        log_total = peak + jnp.log(jnp.sum(jnp.exp(scores - peak), axis=1, keepdims=True))
        probs = jnp.exp(scores - log_total)
        soft = probs.astype(half_type)
        context = dot(soft, values_h)
        delta = jnp.sum(
            upstream_h.astype(f32) * context.astype(half_type).astype(f32), axis=1, keepdims=True
        )
        probs_grad = dot(upstream_h, values, ((1,), (1,)))
        score_grad = (probs * (probs_grad - delta) * scale).astype(half_type)
        results = (
            context,
            dot(score_grad, keys_h),
            dot(score_grad, queries_h, ((0,), (0,))),
            dot(soft, upstream_h, ((0,), (0,))),
        )
        for i, value in enumerate(results):

            @pl.when(h == 0)
            def _():
                heads_sum[i] = value

            @pl.when(h > 0)
            def _():
                heads_sum[i] += value

        @pl.when(h == heads - 1)
        def _():
            back_out[s, :, :cols] = heads_sum[0].astype(half_type)
            for i in range(1, 4):
                value = heads_sum[i]
                if i < 3:
                    value = (
                        value * cosine_ref[...]
                        + pltpu.roll(value * fore_ref[...], cols - ROT // 2, 1)
                        + pltpu.roll(value * aft_ref[...], ROT // 2, 1)
                    )
                back_out[s, :, i * cols : (i + 1) * cols] = value.astype(half_type)
                total = jnp.sum(value, axis=0, keepdims=True)

                @pl.when(s == 0)
                def _():
                    inward_sum[i - 1 : i, :] = total

                @pl.when(s > 0)
                def _():
                    inward_sum[i - 1 : i, :] += total

            for d in range(context_count):
                turn_copy(s, d).start()

    def turn_copy(s, d):
        target = (z + d) % context_count
        source = back_out.at[s, pl.ds(pl.multiple_of(target * tokens, tokens), tokens), :]
        row = pl.multiple_of((z * own_sequences + s) * tokens, tokens)
        destination = back_in.at[pl.ds(row, tokens), :]
        if d == 0:
            return pltpu.make_async_copy(source, destination, own_sems.at[s])
        return remote(source, destination, *sem(turn_sems, s, d - 1), others[d - 1])

    def turned():
        for s in range(own_sequences):
            turn_copy(s, 0).wait()
            for d in range(1, context_count):
                turn_copy(s, d).wait_recv()


    def head_gradients():
        rows = first_rows.shape[0]
        context_rows = back_in[:, :cols]
        delta = dot(context_rows, grads[...], ((0,), (0,))).astype(half_type)
        part[early_rows + 2 * late_other * piece * 2 :, :] = delta
        half = width // 2
        group = cols * half // width
        blocks = width // cols

        def half_rows(s, carry):
            owner = (1 - y) * (1 - s) + y * s
            column = pl.multiple_of(owner * half, half)
            delta = dot(
                first_rows[:, pl.ds(column, half)], back_in[:, cols:], ((0,), (0,))
            ).astype(half_type)
            top = pl.multiple_of(early_rows + s * 3 * group, group)
            for i in range(3):
                for j in range(blocks):
                    part[pl.ds(top + i * group, group), j * cols : (j + 1) * cols] = delta[
                        j * group : (j + 1) * group, i * cols : (i + 1) * cols
                    ]
            return carry

        lax.fori_loop(0, 2, half_rows, 0)

    tile = min(256, plane * tokens)
    tiles = plane * tokens // tile

    def output_rows():
        def step(i, carry):
            rows = pl.ds(pl.multiple_of(i * tile, tile), tile)
            value = dot(back_in[rows, :cols], outward[...])
            out_rows[rows, :] = (out_rows[rows, :].astype(f32) + value).astype(half_type)
            return carry

        lax.fori_loop(0, tiles, step, 0)

    def first_back_rows():
        def step(i, carry):
            scale_total, shift_total = carry
            rows = pl.ds(pl.multiple_of(i * tile, tile), tile)
            value = dot(back_in[rows, cols:], inward[...], ((1,), (1,)))
            first_back[rows, :] = value.astype(half_type)
            normed = (inputs[rows, :].astype(f32) - mean_ref[rows, :]) * inverse_ref[rows, :]
            return (
                scale_total + jnp.sum(value * normed, axis=0, keepdims=True),
                shift_total + jnp.sum(value, axis=0, keepdims=True),
            )

        nothing = jnp.zeros((1, width), f32)
        totals = lax.fori_loop(0, tiles, step, (nothing, nothing))
        lines = width // 128
        vector_sum[len(stages)] = vector_ref[...]
        index = y * batch_count + b
        for i in range(3):
            for j in range(cols // 128):
                line = i * lines + index * (cols // 128) + j
                vector_sum[len(stages), pl.ds(line, 1), :] = inward_sum[
                    i : i + 1, j * 128 : (j + 1) * 128
                ]
        first = vector_ref.shape[0] - 2 * lines
        for i, total in enumerate(totals):
            for j in range(lines):
                line = first + i * lines + j
                vector_sum[len(stages), line : line + 1, :] = total[:, j * 128 : (j + 1) * 128]

    def vector_copy(i):
        source = vector_sum.at[len(stages) if i == 0 else i - 1]
        return remote(source, vector_in.at[i], *sem(vector_sems, i), stages[i])


    arrays = (second_rows, out_rows, first_back)
    block = fsdp_count * tokens

    def near_copy(a, c):
        row = pl.multiple_of((c * CORES + 1 - core) * block, block)
        return remote(
            arrays[a].at[pl.ds(row, block), :],
            near.at[a, pl.ds(c * block, block), :],
            *sem(near_sems, a, c),
            sibling,
        )

    def across_copy(a, c):
        row = pl.multiple_of(c * block + (1 - y) * tokens, tokens)
        return remote(
            near.at[a, pl.ds(row, tokens), :],
            across_in.at[a, pl.ds(c * tokens, tokens), :],
            *sem(across_sems, a, c),
            across,
        )

    def far_copy(a, d):
        row = pl.multiple_of((chip + d + 1) % chips * tokens, tokens)
        return remote(
            across_in.at[a, pl.ds(row, tokens), :], far.at[a, d], *sem(far_sems, a, d), peers[d]
        )

    def scatter_first(a):
        for c in range(chips):
            near_copy(a, c).start()

    def scatter_second(a):
        for c in range(chips):
            near_copy(a, c).wait_recv()

            def step(i, carry):
                row = pl.multiple_of((c * CORES + core) * block + i * tokens, tokens)
                mine = arrays[a][pl.ds(row, tokens), :].astype(f32)
                at = pl.ds(pl.multiple_of(c * block + i * tokens, tokens), tokens)
                near[a, at, :] = (mine + near[a, at, :].astype(f32)).astype(half_type)
                return carry

            lax.fori_loop(0, fsdp_count, step, 0)
            across_copy(a, c).start()

    def scatter_third(a):
        for c in range(chips):
            across_copy(a, c).wait_recv()

        def both(c):
            row = pl.multiple_of(c * block + y * tokens, tokens)
            at = pl.ds(pl.multiple_of(c * tokens, tokens), tokens)
            return (
                near[a, pl.ds(row, tokens), :].astype(f32) + across_in[a, at, :].astype(f32),
                at,
            )

        for d in range(chips - 1):
            value, at = both((chip + d + 1) % chips)
            across_in[a, at, :] = value.astype(half_type)
            far_copy(a, d).start()
        token_sum[a] = both(chip)[0]

    def scatter_last(a):
        value = token_sum[a]
        for d in range(chips - 1):
            far_copy(a, d).wait_recv()
            value = value + far[a, d].astype(f32)
        token_ref[a] = value


    problems = own_sequences * heads
    ready = max(early - 4, problems)
    plan = {}

    def at(slot, work):
        plan.setdefault(slot, []).append(work)

    def scatter(a, slot):
        at(slot, lambda: scatter_first(a))
        at(slot + 3, lambda: scatter_second(a))
        at(slot + 6, lambda: scatter_third(a))
        at(slot + 9, lambda: scatter_last(a))

    at(0, lambda: loads[2].wait())
    scatter(0, 0)
    at(ready, lambda: [load.wait() for load in loads[3:]])
    at(ready, turned)
    at(ready, head_gradients)
    at(ready + 1, output_rows)
    scatter(1, ready + 1)
    at(ready + 2, first_back_rows)
    scatter(2, ready + 2)
    at(ready + 2, lambda: vector_copy(0).start())
    for i in range(len(stages)):

        def vector_step(i=i):
            vector_copy(i).wait_recv()
            before = vector_sum[len(stages) if i == 0 else i - 1]
            vector_sum[i] = before + vector_in[i]
            if i + 1 < len(stages):
                vector_copy(i + 1).start()

        at(ready + 4 + 2 * i, vector_step)

    loads[0].wait()
    loads[1].wait()

    def slot_step(t, carry):
        for half in range(2):
            pieces(t, half)

        @pl.when(t < problems)
        def _():
            attend(t)

        for slot, works in sorted(plan.items()):

            @pl.when(t == slot)
            def _():
                for work in works:
                    work()

        return carry

    slots = max(steps + 2 * last + 4, max(plan) + 1)
    lax.fori_loop(0, slots, slot_step, 0)
    vector_out[...] = vector_sum[len(stages) - 1]

    def drain(k, carry):
        for half in range(2):
            position = z if half == 0 else last - z
            for d in range(chips):
                core_copy(d, half, k, b).wait_recv()
                core_copy(d, half, k, b).wait_send()
                if d:
                    chip_copy(d - 1, half, k, b).wait_send()

            @pl.when(position < last)
            def _():
                row = place(half, k)
                remote(
                    rows_at(reduced, row), rows_at(reduced, row), *sem(reduce_sems, half, k), across
                ).wait_send()

            @pl.when(position > 0)
            def _():
                back_copy(half, k, across).wait_send()

            @pl.when(own(k) == 0)
            def _():
                row_copy(half, k).wait_send()

        return carry

    lax.fori_loop(0, steps, drain, 0)
    store = pltpu.make_async_copy(final.at[pl.ds(0, batch_count)], sums_ref, store_sems)
    store.start()
    for i in range(len(stages)):
        vector_copy(i).wait_send()
    for s in range(own_sequences):
        for d in range(1, context_count):
            turn_copy(s, d).wait_send()
    for a in range(3):
        for c in range(chips):
            near_copy(a, c).wait_send()
            across_copy(a, c).wait_send()
        for d in range(chips - 1):
            far_copy(a, d).wait_send()
    store.wait()


def back_part(
    part,
    mixed,
    out_part,
    second_part,
    first_rows,
    grads,
    inputs,
    mean,
    inverse,
    inward,
    outward,
    places,
    tables,
    vector,
    tokens,
    heads,
    hidden,
):
    sizes = tuple(lax.axis_size(name) for name in ("batch", "ctx", "fsdp"))
    batch_count, context_count, fsdp_count = sizes
    plane = batch_count * fsdp_count
    chips = batch_count // CORES
    width = part.shape[1]
    cols = heads * HEAD_DIM
    length = tokens * context_count
    own_sequences = plane // context_count
    half = width // 2
    unit = hidden // plane
    early_other, early = (unit * half // width, 2 * unit * half // width + unit)
    late_other, late = (3 * cols * half // width, 6 * cols * half // width + cols)
    piece = 32
    for rows in (early_other, early - early_other, late_other, late - late_other):
        piece = math.gcd(piece, rows // 2)
    counts = tuple(n // 2 // piece for n in (early_other, early, late_other, late))
    steps = counts[1] + counts[3]
    rows = early + late
    stage_count = (plane * context_count).bit_length() - 1
    all_tokens = plane * tokens
    dma = pltpu.SemaphoreType.DMA
    f32, half_type = (jnp.float32, part.dtype)
    vmem = pl.BlockSpec(memory_space=pltpu.VMEM)
    hbm = pl.BlockSpec(memory_space=pl.ANY)

    def held(*shape, dtype=half_type):
        return pltpu.VMEM(shape, dtype)

    return pl.pallas_call(
        functools.partial(back_kernel, sizes, tokens, heads, counts, piece),
        out_shape=(
            jax.ShapeDtypeStruct((batch_count, rows, width), half_type),
            jax.ShapeDtypeStruct((3, tokens, width), f32),
            jax.ShapeDtypeStruct(vector.shape, f32),
        ),
        in_specs=[hbm] * 7 + [vmem] * 2 + [hbm] * 2 + [vmem] * 6,
        out_specs=(hbm, vmem, vmem),
        scratch_shapes=[
            held(rows, width),
            held(own_sequences, length, 4 * cols),
            held(all_tokens, width),
            held(all_tokens, width),
            held(all_tokens, width),
            held(all_tokens, width),
            held(all_tokens, width),
            held(all_tokens, width),
            held(width, 3 * cols),
            held(cols, width),
            held(8, 128),
            held(4, length, cols, dtype=f32),
            held(own_sequences, length, 4 * cols),
            held(all_tokens, 4 * cols),
            held(8, cols, dtype=f32),
            held(batch_count + 1, rows, width),
            held(rows, width),
            held(3, chips * fsdp_count * tokens, width),
            held(3, chips * tokens, width),
            held(3, chips - 1, tokens, width),
            held(3, tokens, width, dtype=f32),
            held(stage_count, *vector.shape, dtype=f32),
            held(stage_count + 1, *vector.shape, dtype=f32),
            dma((9,)),
            dma,
            dma((own_sequences,)),
            dma((2, own_sequences, context_count - 1)),
            dma((2, 2, steps)),
            dma((2, 2, steps)),
            dma((2, 2, steps)),
            dma((2, chips - 1, 2, steps)),
            dma((2, chips, 2, steps)),
            dma((2, 3, chips)),
            dma((2, 3, chips)),
            dma((2, 3, chips - 1)),
            dma((2, stage_count)),
        ],
        name="back_part",
        compiler_params=pltpu.CompilerParams(
            collective_id=0, has_side_effects=True, vmem_limit_bytes=VMEM_LIMIT
        ),
    )(
        part,
        mixed,
        out_part,
        second_part,
        first_rows,
        grads,
        inputs,
        mean,
        inverse,
        inward,
        outward,
        *places,
        *tables,
        vector,
    )


def widen_kernel(cols, unit, turn_ref, all_ref, inward_ref, outward_ref, expand_ref, contract_ref,
                 held, inward, outward, expand, contract, in_sems, out_sems):
    batch_count, rows, width = all_ref.shape
    half = inward_ref.shape[0]
    unit_rows, unit_blocks = (unit * half // width, width // unit)
    head_rows, head_blocks = (cols * half // width, width // cols)
    late = 2 * unit_rows + unit
    y = turn_ref[0]

    def load(b):
        return pltpu.make_async_copy(all_ref.at[b], held.at[b % 2], in_sems.at[b % 2])

    def stores(b):
        at = b % 2
        sems = iter(range(2 + 2 * 4))
        out = [
            pltpu.make_async_copy(
                outward.at[at],
                outward_ref.at[pl.ds(b * cols, cols), :],
                out_sems.at[at, next(sems)],
            ),
            pltpu.make_async_copy(
                contract.at[at],
                contract_ref.at[pl.ds(b * unit, unit), :],
                out_sems.at[at, next(sems)],
            ),
        ]
        for s in range(2):
            owner = y if s else 1 - y
            column = pl.multiple_of((owner * batch_count + b) * unit, unit)
            out.append(
                pltpu.make_async_copy(
                    expand.at[at, s],
                    expand_ref.at[:, pl.ds(column, unit)],
                    out_sems.at[at, next(sems)],
                )
            )
            for i in range(3):
                column = pl.multiple_of(i * width + (owner * batch_count + b) * cols, cols)
                out.append(
                    pltpu.make_async_copy(
                        inward.at[at, s, i],
                        inward_ref.at[:, pl.ds(column, cols)],
                        out_sems.at[at, next(sems)],
                    )
                )
        return out

    load(0).start()

    def step(b, carry):
        at = b % 2
        load(b).wait()

        @pl.when(b + 1 < batch_count)
        def _():
            load(b + 1).start()

        @pl.when(b >= 2)
        def _():
            for copy in stores(b - 2):
                copy.wait()

        for s in range(2):
            first = s * unit_rows
            for i in range(unit_blocks):
                expand[at, s, i * unit_rows : (i + 1) * unit_rows, :] = held[
                    at, first : first + unit_rows, i * unit : (i + 1) * unit
                ].astype(jnp.float32)
            for part in range(3):
                top = late + (s * 3 + part) * head_rows
                for i in range(head_blocks):
                    inward[at, s, part, i * head_rows : (i + 1) * head_rows, :] = held[
                        at, top : top + head_rows, i * cols : (i + 1) * cols
                    ].astype(jnp.float32)
        contract[at] = held[at, 2 * unit_rows : late, :].astype(jnp.float32)
        outward[at] = held[at, late + 6 * head_rows :, :].astype(jnp.float32)
        for copy in stores(b):
            copy.start()
        return carry

    lax.fori_loop(0, batch_count, step, 0)
    for b in range(max(0, batch_count - 2), batch_count):
        for copy in stores(b):
            copy.wait()


def widen(gathered, cols, unit, half, hidden):
    batch_count, rows, width = gathered.shape
    turn = lax.axis_index("fsdp").astype(jnp.int32)[None]
    f32 = jnp.float32
    dma = pltpu.SemaphoreType.DMA
    hbm = pl.BlockSpec(memory_space=pl.ANY)
    return pl.pallas_call(
        functools.partial(widen_kernel, cols, unit),
        out_shape=(
            jax.ShapeDtypeStruct((half, 3 * width), f32),
            jax.ShapeDtypeStruct((half, width), f32),
            jax.ShapeDtypeStruct((half, hidden), f32),
            jax.ShapeDtypeStruct((hidden // 2, width), f32),
        ),
        in_specs=[pl.BlockSpec(memory_space=pltpu.SMEM), hbm],
        out_specs=(hbm,) * 4,
        scratch_shapes=[
            pltpu.VMEM((2, rows, width), gathered.dtype),
            pltpu.VMEM((2, 2, 3, half, cols), f32),
            pltpu.VMEM((2, cols, width), f32),
            pltpu.VMEM((2, 2, half, unit), f32),
            pltpu.VMEM((2, unit, width), f32),
            dma((2,)),
            dma((2, 10)),
        ],
        name="widen",
        compiler_params=pltpu.CompilerParams(vmem_limit_bytes=VMEM_LIMIT),
    )(turn, gathered)


def fold(columns, unit, half):
    width = columns.shape[0]
    blocks = width // unit
    parts = columns.reshape(2, blocks, half // blocks, unit).transpose(0, 2, 1, 3)
    return parts.reshape(2, -1, width)


def dot(left, right, contract=((1,), (0,))):
    return lax.dot_general(left, right, (contract, ((), ())), preferred_element_type=jnp.float32)


def normalize(values):
    center = values - jnp.mean(values, axis=-1, keepdims=True)
    inverse = lax.rsqrt(jnp.mean(center * center, axis=-1, keepdims=True) + EPSILON)
    return (center * inverse, inverse)


def norm_backward(upstream, normed, inverse, factor):
    scaled = upstream * factor
    middle = jnp.mean(scaled, axis=-1, keepdims=True)
    coupled = jnp.mean(scaled * normed, axis=-1, keepdims=True)
    result = inverse * (scaled - middle - normed * coupled)
    return (result, jnp.sum(upstream * normed, axis=0), jnp.sum(upstream, axis=0))


def slot_positions(span_order, first_slot, slot_count, span_size):
    slot_index = first_slot + jnp.arange(slot_count, dtype=jnp.int32)
    owners = slot_index // (2 * span_size)
    places = jnp.arange(span_order.shape[0], dtype=jnp.int32)
    leading = jnp.sum(jnp.where(owners[:, None] == places[None, :], span_order[None, :], 0), axis=1)
    spans = 2 * span_order.shape[0]
    picked = jnp.where(slot_index // span_size % 2 == 0, leading, spans - 1 - leading)
    return picked * span_size + slot_index % span_size


def rotary_tables(positions):
    half_rot = ROT // 2
    angular = jnp.exp(
        jnp.arange(half_rot, dtype=jnp.float32) * (-2.0 * math.log(ROTARY_BASE) / ROT)
    )
    angles = positions.astype(jnp.float32)[:, None] * angular[None, :]
    angles = jnp.concatenate([angles, angles], axis=1)
    return (jnp.cos(angles), jnp.sin(angles))


def rotate(tensor, cosine, sine_table):
    half_rot = ROT // 2
    leading_part = tensor[..., :ROT]
    turned = jnp.concatenate([-leading_part[..., half_rot:], leading_part[..., :half_rot]], axis=-1)
    rotated = leading_part * cosine[:, None, :] + turned * sine_table[:, None, :]
    return jnp.concatenate([rotated, tensor[..., ROT:]], axis=-1)


def unrotate(tensor, cosine, sine_table):
    half_rot = ROT // 2
    leading_part = tensor[..., :ROT]
    weighted = leading_part * sine_table[:, None, :]
    turned = jnp.concatenate([weighted[..., half_rot:], -weighted[..., :half_rot]], axis=-1)
    return jnp.concatenate([leading_part * cosine[:, None, :] + turned, tensor[..., ROT:]], axis=-1)


def attention(mixed, place, cosine, sine_table, heads):
    sequences, length, _ = mixed.shape
    parts = mixed.reshape(sequences, length, 4, heads, HEAD_DIM)
    queries, keys, values, grads = (parts[:, :, i] for i in range(4))
    scale = 1.0 / math.sqrt(HEAD_DIM)
    scores = jnp.einsum("sqhd,skhd->shqk", queries, keys, preferred_element_type=jnp.float32)
    allowed = place[None, :] <= place[:, None]
    scores = jnp.where(allowed, scores * scale, MASKED)
    peak = jnp.max(scores, axis=-1, keepdims=True)
    log_total = peak + jnp.log(jnp.sum(jnp.exp(scores - peak), axis=-1, keepdims=True))
    probs = jnp.exp(scores - log_total)
    soft = probs.astype(jnp.bfloat16)
    context = jnp.einsum("shqk,skhd->sqhd", soft, values, preferred_element_type=jnp.float32)
    context = context.astype(jnp.bfloat16)
    delta = jnp.einsum(
        "sqhd,sqhd->shq", grads.astype(jnp.float32), context.astype(jnp.float32)
    )
    value_grad = jnp.einsum("shqk,sqhd->skhd", soft, grads, preferred_element_type=jnp.float32)
    probs_grad = jnp.einsum("sqhd,skhd->shqk", grads, values, preferred_element_type=jnp.float32)
    score_grad = (probs * (probs_grad - delta[..., None]) * scale).astype(jnp.bfloat16)
    query_grad = jnp.einsum("shqk,skhd->sqhd", score_grad, keys, preferred_element_type=jnp.float32)
    key_grad = jnp.einsum("shqk,sqhd->skhd", score_grad, queries, preferred_element_type=jnp.float32)
    query_grad = unrotate(query_grad, cosine, sine_table)
    key_grad = unrotate(key_grad, cosine, sine_table)
    back = jnp.stack([query_grad, key_grad, value_grad], axis=2)
    shift = jnp.sum(back, axis=(0, 1)).reshape(-1)
    full = jnp.concatenate([context[:, :, None], back.astype(jnp.bfloat16)], axis=2)
    return (full.reshape(sequences, length, 4 * heads * HEAD_DIM), shift)


def body(
    layer_input,
    out_grad,
    span_order,
    inward,
    inward_bias,
    outward,
    outward_bias,
    expand,
    expand_bias,
    contract,
    contract_bias,
    first_gain,
    first_bias,
    second_gain,
    second_bias,
):
    batch_count, fsdp_count = (lax.axis_size("batch"), lax.axis_size("fsdp"))
    context_count = lax.axis_size("ctx")
    context_index = lax.axis_index("ctx")
    batch_index, fsdp_index = (lax.axis_index("batch"), lax.axis_index("fsdp"))
    plane = batch_count * fsdp_count
    tokens, width = layer_input.shape[1:]
    hidden_units = expand.shape[1]
    head_cols = width // plane
    unit_cols = hidden_units // plane
    heads = head_cols // HEAD_DIM
    length = tokens * context_count
    span_size = tokens // 2
    own_sequences = plane // context_count

    def full_vectors(*vectors):
        sizes = [v.shape[0] for v in vectors]
        gathered = lax.all_gather(jnp.concatenate(vectors), "fsdp")
        out, start = ([], 0)
        for size in sizes:
            out.append(gathered[:, start : start + size].reshape(-1).astype(jnp.float32))
            start += size
        return out

    (
        inward_offset,
        outward_offset,
        expand_offset,
        contract_offset,
        gain_first,
        offset_first,
        gain_second,
        offset_second,
    ) = full_vectors(
        inward_bias,
        outward_bias,
        expand_bias,
        contract_bias,
        first_gain,
        first_bias,
        second_gain,
        second_bias,
    )

    def chunk(array, cols):
        rows = array.shape[0]
        parts = array.reshape(rows, -1, fsdp_count, batch_count, cols)
        mine = lax.dynamic_index_in_dim(parts, batch_index, 3, keepdims=False)
        return mine.transpose(2, 0, 1, 3).reshape(fsdp_count, rows, -1)

    to_send = jnp.concatenate([chunk(inward, head_cols), chunk(expand, unit_cols)], axis=2)
    weights = lax.all_to_all(to_send, "fsdp", 0, 0).reshape(width, -1)
    inward_cols = weights[:, : 3 * head_cols]
    expand_cols = weights[:, 3 * head_cols :]
    outward_rows = lax.dynamic_slice_in_dim(outward, batch_index * head_cols, head_cols, 0)
    contract_rows = lax.dynamic_slice_in_dim(contract, batch_index * unit_cols, unit_cols, 0)
    plane_index = fsdp_index * batch_count + batch_index
    inward_shift_in = lax.dynamic_index_in_dim(
        inward_offset.reshape(3, plane, head_cols), plane_index, 1, keepdims=False
    ).reshape(-1)
    expand_shift_in = lax.dynamic_slice_in_dim(expand_offset, plane_index * unit_cols, unit_cols, 0)

    pair = jnp.stack([layer_input[0], out_grad[0]])
    pair_all = lax.all_gather(pair, PLANE, axis=1, tiled=True)
    grads_all = pair_all[1]
    rows_all = pair_all[0].astype(jnp.float32)
    normed, inverse = normalize(rows_all)
    first_rows = (normed * gain_first + offset_first).astype(jnp.bfloat16)
    second_rows = (normed * gain_second + offset_second).astype(jnp.bfloat16)

    local_place = slot_positions(span_order, context_index * tokens, tokens, span_size)
    cosine, sine_table = rotary_tables(local_place)
    cosine_plane = jnp.tile(cosine, (plane, 1))
    sine_plane = jnp.tile(sine_table, (plane, 1))
    projected = dot(first_rows, inward_cols) + inward_shift_in
    projected = projected.reshape(plane * tokens, 3 * heads, HEAD_DIM)
    turned = rotate(projected[:, : 2 * heads], cosine_plane, sine_plane)
    context_grad = dot(grads_all, outward_rows, ((1,), (1,)))
    mixed = jnp.concatenate(
        [
            turned.reshape(plane * tokens, -1),
            projected[:, 2 * heads :].reshape(plane * tokens, -1),
            context_grad,
        ],
        axis=1,
    ).astype(jnp.bfloat16)
    mixed = mixed.reshape(context_count, own_sequences, tokens, 4 * head_cols)
    mixed = lax.all_to_all(mixed, "ctx", 0, 0)
    mixed = mixed.transpose(1, 0, 2, 3).reshape(own_sequences, length, 4 * head_cols)
    place = slot_positions(span_order, 0, length, span_size)
    cosine_all, sine_all = rotary_tables(place)

    before = dot(second_rows, expand_cols) + expand_shift_in
    tail = 1.0 + lax.erf(before * HALF_ROOT)
    activated = (0.5 * before * tail).astype(jnp.bfloat16)
    slope = 0.5 * tail + before * jnp.exp(-0.5 * before * before) * NORMAL_PEAK
    before_grad = dot(grads_all, contract_rows, ((1,), (1,))) * slope
    expand_sum = jnp.sum(before_grad, axis=0)
    before_rows = before_grad.astype(jnp.bfloat16)
    expand_delta = dot(second_rows, before_rows, ((0,), (0,)))
    contract_delta = dot(activated, grads_all, ((0,), (0,)))
    out_part = dot(activated, contract_rows)
    second_part = dot(before_rows, expand_cols, ((1,), (1,)))

    hidden = layer_input[0].astype(jnp.float32)
    grad_float = out_grad[0].astype(jnp.float32)
    normed_mine, inverse_mine = normalize(hidden)
    half = width // fsdp_count

    def spread(values, sizes):
        wide = jnp.zeros((sizes[0], plane, sizes[1]), jnp.float32)
        values = values.reshape(sizes[0], sizes[1])
        return lax.dynamic_update_index_in_dim(wide, values, plane_index, 1).reshape(-1)

    bias_total = jnp.sum(grad_float, axis=0)
    expand_wide = spread(expand_sum, (1, unit_cols))

    if head_cols % 128 == 0:
        slots = fold(expand_delta, unit_cols, half).astype(jnp.bfloat16)
        slots = jnp.where(fsdp_index == 0, slots[::-1], slots).reshape(-1, width)
        part = jnp.concatenate([slots, contract_delta.astype(jnp.bfloat16)], axis=0)
        second_sums = [jnp.sum(second_part * normed, axis=0), jnp.sum(second_part, axis=0)]
        nothing = jnp.zeros((width,), jnp.float32)
        inward_wide = jnp.zeros((3 * width,), jnp.float32)
        vectors = [inward_wide, bias_total, expand_wide, *second_sums, nothing, nothing]
        half_rot = ROT // 2
        blank = jnp.zeros((length, HEAD_DIM - ROT), jnp.float32)
        zero = jnp.zeros((length, half_rot), jnp.float32)
        tables = [
            jnp.concatenate([cosine_all, blank + 1.0], axis=1),
            jnp.concatenate([zero, sine_all[:, half_rot:], blank], axis=1),
            jnp.concatenate([-sine_all[:, :half_rot], zero, blank], axis=1),
        ]
        tables = [jnp.tile(table, (1, heads)) for table in tables]
        gathered, mine, whole = back_part(
            part,
            mixed,
            out_part.astype(jnp.bfloat16),
            second_part.astype(jnp.bfloat16),
            first_rows,
            grads_all,
            pair_all[0],
            jnp.mean(rows_all, axis=-1, keepdims=True),
            inverse,
            inward_cols,
            outward_rows,
            (place[:, None], place[None, :]),
            tables,
            jnp.concatenate(vectors).reshape(-1, 128),
            tokens,
            heads,
            hidden_units,
        )
        totals = widen(gathered, head_cols, unit_cols, half, hidden_units)
        whole = whole.reshape(-1)
        order = (0, 1, 2, 5, 6, 3, 4)
    else:
        back, inward_sum = attention(mixed, place, cosine_all, sine_all, heads)
        back = back.reshape(own_sequences, context_count, tokens, 4 * head_cols)
        back = lax.all_to_all(back.transpose(1, 0, 2, 3), "ctx", 0, 0)
        back = back.reshape(plane * tokens, 4 * head_cols)
        context_rows = back[:, :head_cols]
        projected_rows = back[:, head_cols:]
        inward_delta = dot(first_rows, projected_rows, ((0,), (0,)))
        outward_delta = dot(context_rows, grads_all, ((0,), (0,)))
        out_part = out_part + dot(context_rows, outward_rows)
        first_part = dot(projected_rows, inward_cols, ((1,), (1,)))
        stacked = jnp.stack([second_part, out_part, first_part], axis=1).astype(jnp.bfloat16)
        mine = lax.psum_scatter(stacked, PLANE, scatter_dimension=0, tiled=True)
        mine = mine.transpose(1, 0, 2).astype(jnp.float32)
        columns = jnp.concatenate([inward_delta, expand_delta], axis=1).astype(jnp.bfloat16)
        rows = jnp.concatenate([outward_delta, contract_delta], axis=0).astype(jnp.bfloat16)
        columns, rows = lax.psum((columns, rows), "ctx")
        columns = lax.all_to_all(columns.reshape(fsdp_count, half, -1), "fsdp", 0, 0)
        columns = lax.all_gather(columns, "batch")
        rows = lax.all_gather(rows, "batch").astype(jnp.float32)
        columns = columns.transpose(2, 1, 0, 3).astype(jnp.float32)
        inward_total = columns[..., : 3 * head_cols].reshape(
            half, fsdp_count, batch_count, 3, head_cols
        )
        totals = (
            inward_total.transpose(0, 3, 1, 2, 4).reshape(half, 3 * width),
            rows[:, :head_cols].reshape(half, width),
            columns[..., 3 * head_cols :].reshape(half, hidden_units),
            rows[:, head_cols:].reshape(-1, width),
        )
        _, second_scale, second_shift = norm_backward(
            mine[0], normed_mine, inverse_mine, gain_second
        )
        _, first_scale, first_shift = norm_backward(mine[2], normed_mine, inverse_mine, gain_first)
        vectors = [
            spread(inward_sum, (3, head_cols)),
            bias_total,
            expand_wide,
            first_scale,
            first_shift,
            second_scale,
            second_shift,
        ]
        whole = lax.psum(jnp.concatenate(vectors), ("batch", "ctx", "fsdp"))
        order = tuple(range(7))

    result = (hidden + (mine[1] + outward_offset) + contract_offset).astype(jnp.bfloat16)
    second_input, _, _ = norm_backward(mine[0], normed_mine, inverse_mine, gain_second)
    first_input, _, _ = norm_backward(mine[2], normed_mine, inverse_mine, gain_first)
    input_delta = grad_float + first_input + second_input
    halves, start = ([], 0)
    for vector in vectors:
        size = vector.shape[0] // fsdp_count
        halves.append(lax.dynamic_slice_in_dim(whole, start + fsdp_index * size, size, 0))
        start += vector.shape[0]
    halves = [halves[i] for i in order]
    return (
        result[None],
        input_delta[None],
        totals[0],
        halves[0],
        totals[1],
        halves[1],
        totals[2],
        halves[2],
        totals[3],
        halves[1],
        halves[3],
        halves[4],
        halves[5],
        halves[6],
    )


def solution(mesh):
    rows = P(PLANE, "ctx", None)
    matrix, vector = (P("fsdp", None), P("fsdp"))
    in_specs = (rows, rows, P()) + (matrix, vector) * 4 + (vector,) * 4
    out_specs = (rows, rows) + (matrix, vector) * 4 + (vector,) * 4
    return jax.shard_map(body, mesh=mesh, in_specs=in_specs, out_specs=out_specs, check_vma=False)
```

profile of v0, /device:TPU:0, one launch (start us, length us, event | category | flops | bytes accessed | tf_op | source)
XLA Modules:
  0.0 338.6 jit_solution(15900709756035223847)
XLA Ops:
  7.2 2.0 pad_maximum_fusion.3
  9.2 4.6 %copy.82 = bf16[512,3072]{0,1:T(8,128)(2,1)} copy(bf16[512,3072]{1,0:T(8,128)(2,1)} %param.18) | data formatting | bytes 6291456 | tf_op args[3]
  13.9 1.2 dynamic-slice_bitcast_fusion
  15.5 8.0 %reshape.640 = bf16[512,1,2,4,512]{4,3,2,0,1:T(4,128)(2,1)} reshape(bf16[512,4096]{1,0:T(8,128)(2,1)} %param.22) | data formatting | bytes 8388608 | tf_op jit(solution)/shard_map/reshape | solution.py:1011
  23.5 4.3 %constant_dynamic-slice_fusion.1 = bf16[512,1,2,1,512]{4,3,2,0,1:T(2,128)(2,1)S(1)} fusion(bf16[512,1,2,4,512]{4,3,2,0,1:T(4,128)(2,1)} %reshape.640, s32[]{:T(128)S(6)} %select_n.211), kind=kLoop, calls=%fused_computation.178 | loop fusion | bytes 2097156 | tf_op jit(solution)/shard_map/jit(dynamic_index_in_dim)/dynamic_slice | solution.py:1012
  28.2 1.4 pad_maximum_fusion.1
  29.6 4.3 %all-to-all-start = ((bf16[2,512,896]{2,1,0:T(8,128)(2,1)}), bf16[2,512,896]{2,1,0:T(8,128)(2,1)S(1)}, u32[]{:S(2)}, u32[]{:S(2)}) async-start(bf16[2,512,896]{2,1,0:T(8,128)(2,1)} %pad_maximum_fusion.1), calls=%async_computation | async-start | bytes 3670016 | tf_op jit(solution)/shard_map/all_to_all | solution.py:1016
  35.4 33.0 %all-gather.1 = bf16[2,1,6656]{2,1,0:T(2,128)(2,1)S(1)} all-gather(bf16[1,1,6656]{2,1,0:T(2,128)(2,1)S(1)} %reshape.658), channel_id=2, replica_groups=mesh['batch'=4,'ctx'=4,'fsdp'=2] {'fsdp'}, dimensions={0}, use_global_device_ids=true | all-gather | bytes 39936 | tf_op jit(solution)/shard_map/all_gather | solution.py:982
  68.5 0.6 reshape.654
  69.1 0.6 copy.107
  69.8 0.6 copy.114
  70.3 0.6 copy.109
  70.9 0.6 copy.106
  72.2 0.7 tile.47
  72.9 1.8 copy.97.cosine_ref
  74.9 0.7 tile.51
  75.6 1.8 copy.99.aft_ref
  77.4 0.6 broadcast_dynamic-update-slice_fusion
  78.1 0.6 constant_dynamic-update-slice_fusion.5
  78.6 0.7 select_reduce_fusion.1
  79.4 0.7 broadcast_multiply_fusion.1
  80.1 0.6 fusion.63
  81.5 0.9 copy.98.fore_ref
  82.5 0.8 dynamic_slice.45
  83.3 0.7 dynamic-slice_reduce_fusion
  84.5 0.6 fusion.66.place_row
  85.1 0.7 tile.20
  85.8 0.7 tile.22
  86.6 0.8 fusion.55.place_col
  87.3 1.0 slice.104.inward_in
  88.3 2.1 convert_reduce_fusion
  90.4 2.3 fusion.10
  92.7 2.5 multiply_convert_fusion
  95.2 3.9 %fusion.93 = (f32[512]{0:T(512)}, bf16[1024,512]{1,0:T(8,128)(2,1)S(1)}) fusion(f32[1024,512]{1,0:T(8,128)S(1)} %get-tuple-element.64, f32[512]{0:T(512)S(1)} %dynamic_slice.45, bf16[2048,1024]{1,0:T(8,128)(2,1)} %param.24, s32[]{:T(128)S(6)} %select_n.210, bf16[2,1024,1024]{2,1,0:T(8,128)(2,1)S(1)} %copy-done.2), kind=kOutput, calls=%fused_computation.207 | convolution fusion | flops 1080032768 | bytes 6295556 | tf_op jit(solution)/shard_map/dot_general | solution.py:866
  99.1 4.3 %fusion.91 = (f32[1024]{0:T(1024)}, f32[1024]{0:T(1024)}, bf16[1024,1024]{1,0:T(8,128)(2,1)S(1)}, bf16[1024,1024]{0,1:T(8,128)(2,1)}, bf16[1024,1024]{1,0:T(8,128)(2,1)}) fusion(f32[1024]{0:T(1024)S(1)} %add_rsqrt_fusion, f32[1024]{0:T(1024)S(1)} %broadcast_multiply_fusion.2, bf16[2,1024,1024]{2,1,0:T(8,128)(2,1)S(1)} %copy-done.2, ...), kind=kOutput, calls=%fused_computation.205 | convolution fusion | flops 1087371264 | bytes 10518528 | tf_op jit(solution)/shard_map/dot_general | solution.py:866
  103.4 1.0 convolution_add_fusion
  105.5 3.9 %copy.102 = bf16[1024,1024]{1,0:T(8,128)(2,1)} copy(bf16[1024,1024]{0,1:T(8,128)(2,1)} %get-tuple-element.35) | data formatting | bytes 4194304 | tf_op jit(solution)/shard_map/dot_general | solution.py:866
  109.5 4.8 %slice_bitcast_fusion = (bf16[1024,1024]{1,0:T(8,128)(2,1)}, bf16[1024,1024]{1,0:T(8,128)(2,1)}, bf16[1,1024,1024]{2,1,0:T(8,128)(2,1)S(1)}) fusion(bf16[2,1024,1024]{2,1,0:T(8,128)(2,1)} %all-gather.4.cloned.1.call-done), kind=kLoop, calls=%fused_computation.19 | loop fusion | bytes 10485760 | tf_op jit(solution)/shard_map/squeeze | solution.py:1030
  114.3 0.8 convolution_convert_fusion.3
  115.4 1.5 pad_maximum_fusion.2
  116.9 1.7 copy.91
  118.7 4.7 %all-to-all-start.1 = ((bf16[4,2,128,512]{2,1,3,0:T(2,128)(2,1)}), bf16[4,2,128,512]{2,1,3,0:T(2,128)(2,1)S(1)}, u32[]{:S(2)}, u32[]{:S(2)}) async-start(bf16[4,2,128,512]{2,1,3,0:T(2,128)(2,1)} %copy.91), calls=%async_computation.1 | async-start | bytes 2097152 | tf_op jit(solution)/shard_map/all_to_all | solution.py:1052
  123.4 2.9 fusion.16
  126.3 1.0 copy.96.inverse_ref
  127.3 1.0 copy.95.mean_ref
  128.6 0.5 copy.88
  129.4 0.5 copy.89
  129.9 0.6 constant_dynamic-update-slice_fusion.6
  130.5 0.6 constant_dynamic-update-slice_fusion.4
  131.1 0.6 constant_dynamic-update-slice_fusion.3
  131.7 0.6 constant_dynamic-update-slice_fusion.2
  132.3 3.2 convolution_convert_fusion.1
  135.5 1.5 pad_maximum_fusion.part_in
  137.0 3.8 %convolution_convert_fusion.out_in = bf16[1024,1024]{1,0:T(8,128)(2,1)} fusion(bf16[1024,512]{1,0:T(8,128)(2,1)S(1)} %copy-done.31, bf16[2048,1024]{1,0:T(8,128)(2,1)} %param.24, s32[]{:T(128)S(6)} %select_n.210), kind=kOutput, calls=%fused_computation.23 | convolution fusion | flops 1074790400 | bytes 4194308 | tf_op jit(solution)/shard_map/dot_general | solution.py:866
  140.8 8.1 %all-to-all-done.1 = bf16[4,2,128,512]{2,1,3,0:T(2,128)(2,1)S(1)} async-done(((bf16[4,2,128,512]{2,1,3,0:T(2,128)(2,1)}), bf16[4,2,128,512]{2,1,3,0:T(2,128)(2,1)S(1)}, u32[]{:S(2)}, u32[]{:S(2)}) %all-to-all-start.1) | async-done | bytes 1048608 | tf_op jit(solution)/shard_map/all_to_all | solution.py:1052
  148.9 2.0 copy.92
  151.0 156.1 %back_part.1 = (bf16[4,1536,1024]{2,1,0:T(8,128)(2,1)}, f32[3,128,1024]{2,1,0:T(8,128)}, f32[96,128]{1,0:T(8,128)}) custom-call(bf16[1024,1024]{1,0:T(8,128)(2,1)} %pad_maximum_fusion.part_in, bf16[2,512,512]{2,1,0:T(8,128)(2,1)} %bitcast.151, bf16[1024,1024]{1,0:T(8,128)(2,1)} %convolution_convert_fusion.out_in, ...), custom_call_target="tpu_custom_call" | custom-call | tf_op jit(solution)/shard_map/back_part/pallas_call | solution.py:672
  307.0 1.5 fusion.32
  308.6 1.3 dynamic_slice.50
  309.9 1.4 dynamic_slice.48
  311.3 1.4 fusion.92
  312.7 17.1 %widen.1 = (f32[512,3072]{1,0:T(8,128)}, f32[512,1024]{1,0:T(8,128)}, f32[512,4096]{1,0:T(8,128)}, f32[2048,1024]{1,0:T(8,128)}) custom-call(s32[1]{0:T(128)} %bitcast.36.turn_ref, bf16[4,1536,1024]{2,1,0:T(8,128)(2,1)} %get-tuple-element.22.all_ref), custom_call_target="tpu_custom_call" | custom-call | tf_op jit(solution)/shard_map/widen/pallas_call | solution.py:834
  329.9 1.3 fusion.24
  331.1 0.6 copy.136
  (134 shorter events, 6.5 us)
Async XLA Ops:
  7.2 73.6 %copy-start = (bf16[512,1024]{1,0:T(8,128)(2,1)S(1)}, bf16[512,1024]{1,0:T(8,128)(2,1)}, u32[]{:S(2)}) copy-start(bf16[512,1024]{1,0:T(8,128)(2,1)} %param.20) | copy-start | bytes 3145732
  7.2 81.1 %all-gather.4.cloned.1.call-start = ((), (), s32[]{:S(2)}) async-start(), calls=%async_computation.2 | async-start | bytes 4718592 | tf_op jit(solution)/shard_map/all_gather | solution.py:1028
  29.6 4.4 %copy-start.15 = (bf16[1536]{0:T(1024)(128)(2,1)S(1)}, bf16[1536]{0:T(1024)(128)(2,1)}, u32[]{:S(2)}) copy-start(bf16[1536]{0:T(1024)(128)(2,1)} %param.19) | copy-start | bytes 9220
  29.6 4.7 %copy-start.25 = (bf16[512]{0:T(512)(128)(2,1)S(1)}, bf16[512]{0:T(512)(128)(2,1)}, u32[]{:S(2)}) copy-start(bf16[512]{0:T(512)(128)(2,1)} %param.21) | copy-start | bytes 3076
  29.6 4.9 %copy-start.16 = (bf16[2048]{0:T(1024)(128)(2,1)S(1)}, bf16[2048]{0:T(1024)(128)(2,1)}, u32[]{:S(2)}) copy-start(bf16[2048]{0:T(1024)(128)(2,1)} %param.23) | copy-start | bytes 12292
  29.6 4.9 %copy-start.26 = (bf16[512]{0:T(512)(128)(2,1)S(1)}, bf16[512]{0:T(512)(128)(2,1)}, u32[]{:S(2)}) copy-start(bf16[512]{0:T(512)(128)(2,1)} %param.25) | copy-start | bytes 3076
  29.6 5.2 %copy-start.27 = (bf16[512]{0:T(512)(128)(2,1)S(1)}, bf16[512]{0:T(512)(128)(2,1)}, u32[]{:S(2)}) copy-start(bf16[512]{0:T(512)(128)(2,1)} %param.26) | copy-start | bytes 3076
  29.6 5.4 %copy-start.28 = (bf16[512]{0:T(512)(128)(2,1)S(1)}, bf16[512]{0:T(512)(128)(2,1)}, u32[]{:S(2)}) copy-start(bf16[512]{0:T(512)(128)(2,1)} %param.27) | copy-start | bytes 3076
  29.6 5.6 %copy-start.29 = (bf16[512]{0:T(512)(128)(2,1)S(1)}, bf16[512]{0:T(512)(128)(2,1)}, u32[]{:S(2)}) copy-start(bf16[512]{0:T(512)(128)(2,1)} %param.28) | copy-start | bytes 3076
  29.6 5.8 %copy-start.24 = (bf16[512]{0:T(512)(128)(2,1)S(1)}, bf16[512]{0:T(512)(128)(2,1)}, u32[]{:S(2)}) copy-start(bf16[512]{0:T(512)(128)(2,1)} %param.29) | copy-start | bytes 3076
  29.6 41.9 %copy-start.30 = (s32[4]{0:T(128)S(1)}, s32[4]{0:T(128)}, u32[]{:S(2)}) copy-start(s32[4]{0:T(128)} %param.17) | copy-start | bytes 52
  29.6 57.7 %all-to-all-start = ((bf16[2,512,896]{2,1,0:T(8,128)(2,1)}), bf16[2,512,896]{2,1,0:T(8,128)(2,1)S(1)}, u32[]{:S(2)}, u32[]{:S(2)}) async-start(bf16[2,512,896]{2,1,0:T(8,128)(2,1)} %pad_maximum_fusion.1), calls=%async_computation | async-start | bytes 3670016 | tf_op jit(solution)/shard_map/all_to_all | solution.py:1016
  33.9 44.1 %copy-start.6 = (bf16[1,128,1024]{2,1,0:T(8,128)(2,1)S(1)}, bf16[1,128,1024]{2,1,0:T(8,128)(2,1)}, u32[]{:S(2)}) copy-start(bf16[1,128,1024]{2,1,0:T(8,128)(2,1)} %param.16) | copy-start | bytes 786436
  33.9 46.9 %copy-start.3 = (bf16[1,128,1024]{2,1,0:T(8,128)(2,1)S(1)}, bf16[1,128,1024]{2,1,0:T(8,128)(2,1)}, u32[]{:S(2)}) copy-start(bf16[1,128,1024]{2,1,0:T(8,128)(2,1)} %param.15) | copy-start | bytes 786436
  71.5 0.5 copy-start.22
  80.8 33.5 %copy-start.5 = (bf16[128,1024]{1,0:T(8,128)(2,1)}, bf16[128,1024]{1,0:T(8,128)(2,1)S(1)}, u32[]{:S(2)}) copy-start(bf16[128,1024]{1,0:T(8,128)(2,1)S(1)} %constant_dynamic-slice_fusion.outward_in) | copy-start | bytes 786436
  81.0 0.5 copy-start.13
  88.3 4.4 %copy-start.18 = (f32[1,4,2,128]{3,1,2,0:T(4,128)S(1)}, f32[1,4,2,128]{3,1,2,0:T(4,128)}, u32[]{:S(2)}) copy-start(f32[1,4,2,128]{3,1,2,0:T(4,128)} %copy.106) | copy-start | bytes 12292
  88.3 4.4 %copy-start.2 = (bf16[2,1024,1024]{2,1,0:T(8,128)(2,1)S(1)}, bf16[2,1024,1024]{2,1,0:T(8,128)(2,1)}, u32[]{:S(2)}) copy-start(bf16[2,1024,1024]{2,1,0:T(8,128)(2,1)} %all-gather.4.cloned.1.call-done) | copy-start | bytes 12582916
  92.7 6.4 %copy-start.10 = (f32[1024]{0:T(1024)}, f32[1024]{0:T(1024)S(1)}, u32[]{:S(2)}) copy-start(f32[1024]{0:T(1024)S(1)} %add_rsqrt_fusion) | copy-start | bytes 12292
  95.2 3.9 %copy-start.17 = (f32[1,4,2,128]{3,1,2,0:T(4,128)S(1)}, f32[1,4,2,128]{3,1,2,0:T(4,128)}, u32[]{:S(2)}) copy-start(f32[1,4,2,128]{3,1,2,0:T(4,128)} %copy.109) | copy-start | bytes 12292
  99.1 4.3 %copy-start.32 = (bf16[1024,512]{1,0:T(8,128)(2,1)}, bf16[1024,512]{1,0:T(8,128)(2,1)S(1)}, u32[]{:S(2)}) copy-start(bf16[1024,512]{1,0:T(8,128)(2,1)S(1)} %get-tuple-element.66) | copy-start | bytes 3145732
  103.4 1.3 copy-start.8
  118.7 4.7 %copy-start.33 = (bf16[1024,512]{1,0:T(8,128)(2,1)S(1)}, bf16[1024,512]{1,0:T(8,128)(2,1)}, u32[]{:S(2)}) copy-start(bf16[1024,512]{1,0:T(8,128)(2,1)} %copy-done.32) | copy-start | bytes 3145732
  118.7 30.3 %all-to-all-start.1 = ((bf16[4,2,128,512]{2,1,3,0:T(2,128)(2,1)}), bf16[4,2,128,512]{2,1,3,0:T(2,128)(2,1)S(1)}, u32[]{:S(2)}, u32[]{:S(2)}) async-start(bf16[4,2,128,512]{2,1,3,0:T(2,128)(2,1)} %copy.91), calls=%async_computation.1 | async-start | bytes 2097152 | tf_op jit(solution)/shard_map/all_to_all | solution.py:1052
  123.4 2.9 copy-start.11
  123.4 5.0 %copy-start.23 = (f32[512]{0:T(512)S(1)}, f32[512]{0:T(512)}, u32[]{:S(2)}) copy-start(f32[512]{0:T(512)} %get-tuple-element.65) | copy-start | bytes 6148
  129.2 1.4 copy-start.20
  129.2 1.9 copy-start.19
  135.5 1.5 copy-start.31
  150.9 156.1 %copy-start.14 = (f32[128]{0:T(128)S(1)}, f32[128]{0:T(128)}, u32[]{:S(2)}) copy-start(f32[128]{0:T(128)} %copy-done.13) | copy-start | bytes 1540
  151.0 156.1 %copy-start.21 = (f32[128]{0:T(128)S(1)}, f32[128]{0:T(128)}, u32[]{:S(2)}) copy-start(f32[128]{0:T(128)} %add_rsqrt_fusion.1) | copy-start | bytes 1540
  312.7 18.4 %copy-start.12 = (f32[512]{0:T(512)}, f32[512]{0:T(512)S(1)}, u32[]{:S(2)}) copy-start(f32[512]{0:T(512)S(1)} %get-tuple-element.94) | copy-start | bytes 6148
  312.7 17.1 %copy-start.4 = (f32[3,128,1024]{2,1,0:T(8,128)S(1)}, f32[3,128,1024]{2,1,0:T(8,128)}, u32[]{:S(2)}) copy-start(f32[3,128,1024]{2,1,0:T(8,128)} %get-tuple-element.21) | copy-start | bytes 4718596
  312.7 17.2 %copy-start.7 = (bf16[1,128,1024]{2,1,0:T(8,128)(2,1)S(1)}, bf16[1,128,1024]{2,1,0:T(8,128)(2,1)}, u32[]{:S(2)}) copy-start(bf16[1,128,1024]{2,1,0:T(8,128)(2,1)} %param.16) | copy-start | bytes 786436
  312.7 17.2 %copy-start.9 = (f32[1,4,2,128]{3,1,2,0:T(4,128)S(1)}, f32[1,4,2,128]{3,1,2,0:T(4,128)}, u32[]{:S(2)}) copy-start(f32[1,4,2,128]{3,1,2,0:T(4,128)} %copy.114) | copy-start | bytes 12292
  312.7 19.0 %copy-start.1 = (bf16[512,1024]{1,0:T(8,128)(2,1)S(1)}, bf16[512,1024]{1,0:T(8,128)(2,1)}, u32[]{:S(2)}) copy-start(bf16[512,1024]{1,0:T(8,128)(2,1)} %param.20) | copy-start | bytes 3145732
Sparse Core Ops, SparseCore 0:
  10.5 50.4 all-gather.3
where the time goes:
time: 340 us; the launch traced here: 339 us
  Pallas kernels  173 us (51%)
  local copies, waits for them, and re-layouts  59.5 us (18%)
  blocking collectives  33 us (10%)
  matrix products  22.4 us (7%)
  other arithmetic  18.7 us (6%)
  between operations  14.6 us (4%)
  starting transfers between devices  9.06 us (3%)
  waiting for transfers between devices  8.13 us (2%)
    pallas_call x1, Pallas kernels, back_part(): pl.pallas_call(functools.partial(back_kernel, sizes, tokens, heads, count...  156 us
    all_gather x1, blocking collectives, full_vectors(): gathered = lax.all_gather(jnp.concatenate(vectors), 'fsdp')  33 us
    dot_general x8, matrix products, dot(): lax.dot_general(left, right, (contract, ((), ())), preferred_element_type...  22.4 us
    pallas_call x1, Pallas kernels, widen(): pl.pallas_call(functools.partial(widen_kernel, cols, unit), out_shape=(ja...  17.1 us
    unnamed x92, local copies, waits for them, and re-layouts  13.2 us
    all_to_all x1, waiting for transfers between devices, body(): mixed = lax.all_to_all(mixed, 'ctx', 0, 0)  8.11 us
    reshape x1, local copies, waits for them, and re-layouts, chunk(): parts = array.reshape(rows, -1, fsdp_count, batch_count, cols)  7.98 us
  transfers between devices with their start and end apart: 3, of which 1 were waited for; matrix products, arithmetic and copies ran while one was open for 17% of the time, Pallas kernels for 0%

commit v1 on v0

--- a/solution.py
+++ b/solution.py
@@ -50,49 +50,52 @@
     )
 
 
-def back_kernel(
+LAG = 2
+
+
+def layer_kernel(
     sizes,
     tokens,
     heads,
     counts,
     piece,
-    part_in,
-    mixed_in,
-    out_in,
-    second_in,
-    first_rows_in,
-    grads_in,
-    inputs_in,
-    mean_ref,
-    inverse_ref,
-    inward_in,
-    outward_in,
-    place_col,
-    place_row,
-    cosine_ref,
-    fore_ref,
-    aft_ref,
-    vector_ref,
+    input_ref,
+    grad_ref,
+    order_ref,
+    small_ref,
+    inward_ref,
+    outward_ref,
+    expand_ref,
+    contract_ref,
     sums_ref,
-    token_ref,
-    vector_out,
-    part,
-    mixed,
-    out_rows,
-    second_rows,
-    first_back,
-    first_rows,
+    result_ref,
+    input_grad_ref,
+    shifts_ref,
+    inputs,
     grads,
-    inputs,
+    small,
     inward,
     outward,
-    attended,
+    expand,
+    contract,
+    cosine,
+    sine,
+    stats,
+    first_rows,
+    second_rows,
+    work,
+    out_rows,
+    second_back,
+    mixed_out,
+    mixed,
     heads_sum,
     back_out,
     back_in,
     inward_sum,
-    final,
+    part,
+    mine,
     reduced,
+    reduced_right,
     near,
     across_in,
     far,
@@ -100,14 +103,22 @@
     vector_in,
     vector_sum,
     load_sems,
-    store_sems,
-    own_sems,
+    small_sems,
+    weight_sems,
+    gather_sems,
+    share_sems,
+    there_sends,
+    there_recvs,
+    there_own,
+    back_own,
     turn_sems,
     reduce_sems,
-    back_sems,
+    back_sends,
+    back_recvs,
     row_sems,
     chip_sems,
     core_sems,
+    keep_sems,
     near_sems,
     across_sems,
     far_sems,
@@ -120,14 +131,19 @@
     core = b % CORES
     chip = b // CORES
     width = part.shape[1]
+    half_width = width // 2
     cols = heads * HEAD_DIM
+    unit = contract.shape[0]
     plane = batch_count * fsdp_count
+    index = y * batch_count + b
     own_sequences = plane // context_count
     length = tokens * context_count
     steps = early + late
     early_rows = 2 * early * piece
     last = context_count - 1
+    lines = width // 128
     f32, half_type = (jnp.float32, part.dtype)
+    group_rows = fsdp_count * tokens
 
     sibling = (chip * CORES + (1 - core), z, y)
     across = (b, z, 1 - y)
@@ -145,28 +161,304 @@
         stages.append((b, swapped(z, step), y))
         step *= 2
 
-    loads = [
-        pltpu.make_async_copy(source, target, load_sems.at[i])
-        for i, (source, target) in enumerate(
-            [
-                (part_in, part.at[pl.ds(0, early_rows), :]),
-                (mixed_in, mixed),
-                (second_in, second_rows),
-                (out_in, out_rows),
-                (first_rows_in, first_rows),
-                (grads_in, grads),
-                (inputs_in, inputs),
-                (inward_in, inward),
-                (outward_in, outward),
-            ]
+    def sem(sems, *index):
+        return (sems.at[(0, *index)], sems.at[(1, *index)])
+
+
+    plane_arrays = (inputs, grads)
+    plane_sources = (input_ref.at[0], grad_ref.at[0])
+
+    def block(array, batch, fsdp):
+        row = pl.multiple_of((batch * fsdp_count + fsdp) * tokens, tokens)
+        return plane_arrays[array].at[pl.ds(row, tokens), :]
+
+    def own_load(array):
+        return pltpu.make_async_copy(
+            plane_sources[array], block(array, b, y), load_sems.at[array]
         )
+
+    def to_across(array):
+        return remote(
+            plane_sources[array], block(array, b, y), *sem(gather_sems, array, 0), across
+        )
+
+    def to_peer(array, d):
+        return remote(
+            plane_sources[array], block(array, b, y), *sem(gather_sems, array, 1 + d), peers[d]
+        )
+
+    def on_to_peer(array, d):
+        at = block(array, b, 1 - y)
+        return remote(at, at, *sem(gather_sems, array, chips + d), peers[d])
+
+    def share(array, i):
+        if i == 0:
+            return remote(
+                plane_sources[array], block(array, b, y), *sem(share_sems, array, 0), sibling
+            )
+        if i == 1:
+            at = block(array, b, 1 - y)
+        else:
+            d = (i - 2) % (chips - 1)
+            at = block(array, sources[d], y if i - 2 < chips - 1 else 1 - y)
+        return remote(at, at, *sem(share_sems, array, i), sibling)
+
+    def weight_copies(owner, local):
+        rows = pl.ds(pl.multiple_of(y * half_width, half_width), half_width)
+        place = owner * batch_count + b
+        out = []
+        for i in range(4):
+            if i < 3:
+                column = pl.multiple_of(i * width + place * cols, cols)
+                source = inward_ref.at[:, pl.ds(column, cols)]
+                target = inward.at[rows, i * cols : (i + 1) * cols]
+            else:
+                column = pl.multiple_of(place * unit, unit)
+                source = expand_ref.at[:, pl.ds(column, unit)]
+                target = expand.at[rows, :]
+            if local:
+                out.append(pltpu.make_async_copy(source, target, load_sems.at[2 + i]))
+            else:
+                out.append(remote(source, target, *sem(weight_sems, i), across))
+        return out
+
+    row_loads = [
+        pltpu.make_async_copy(
+            outward_ref.at[pl.ds(pl.multiple_of(b * cols, cols), cols), :],
+            outward,
+            load_sems.at[6],
+        ),
+        pltpu.make_async_copy(
+            contract_ref.at[pl.ds(pl.multiple_of(b * unit, unit), unit), :],
+            contract,
+            load_sems.at[7],
+        ),
     ]
-    for load in loads:
+    weight_loads = weight_copies(y, True)
+    weight_sends = weight_copies(1 - y, False)
+    small_copy = remote(small_ref, small.at[1], *sem(small_sems, 0), across)
+
+    own_load(0).start()
+    own_load(1).start()
+    for load in weight_loads + row_loads:
         load.start()
     greet([sibling, across] + peers + others)
-
-    def sem(sems, *index):
-        return (sems.at[(0, *index)], sems.at[(1, *index)])
+    small_copy.start()
+    for array in range(2):
+        to_across(array).start()
+        for d in range(chips - 1):
+            to_peer(array, d).start()
+        share(array, 0).start()
+        if array == 0:
+            for send in weight_sends[:3]:
+                send.start()
+    weight_sends[3].start()
+    small[0] = small_ref[...]
+
+
+    def positions(shape, dimension):
+        slot = lax.broadcasted_iota(jnp.int32, shape, dimension)
+        owner = slot // tokens
+        leading = jnp.zeros(shape, jnp.int32)
+        for c in range(context_count):
+            leading = jnp.where(owner == c, order_ref[c], leading)
+        span = tokens // 2
+        second = slot // span % 2
+        picked = jnp.where(second == 0, leading, 2 * context_count - 1 - leading)
+        return picked * span + slot % span
+
+    half_rot = ROT // 2
+    lane = lax.broadcasted_iota(jnp.int32, (1, cols), 1) % HEAD_DIM
+    angular = jnp.exp((lane % half_rot).astype(f32) * (-2.0 * math.log(ROTARY_BASE) / ROT))
+    angles = positions((length, cols), 0).astype(f32) * angular
+    cosine[...] = jnp.where(lane < ROT, jnp.cos(angles), 1.0)
+    sine[...] = jnp.where(lane < ROT, jnp.sin(angles), 0.0)
+    low = (lane < half_rot).astype(f32)
+    high = 1.0 - low
+
+    def turn(value, rows, sign):
+        weight = sine[rows, :] * sign
+        return (
+            value * cosine[rows, :]
+            - pltpu.roll(value, cols - half_rot, 1) * (weight * low)
+            + pltpu.roll(value, half_rot, 1) * (weight * high)
+        )
+
+
+    small_copy.wait_recv()
+    vector_rows = [3 * lines, lines, unit * plane // 128] + [lines] * 5
+    starts = [sum(vector_rows[:i]) // fsdp_count for i in range(8)]
+
+    def vector_line(which, line):
+        share_lines = vector_rows[which] // fsdp_count
+        owner = line // share_lines
+        at = (owner - y) * (owner - y)
+        return small[at, pl.ds(starts[which] + line % share_lines, 1), :]
+
+    def whole(which):
+        return jnp.concatenate([vector_line(which, line) for line in range(lines)], axis=1)
+
+    def chunk(which, first, count):
+        return jnp.concatenate([vector_line(which, first + i) for i in range(count)], axis=1)
+
+
+    def group(u):
+        return (chip + u // CORES) % chips * CORES + (core + u % CORES) % CORES
+
+    def rows_of(u):
+        return pl.ds(pl.multiple_of(group(u) * group_rows, group_rows), group_rows)
+
+    def bring(array, u):
+        distance, other = (u // CORES, u % CORES)
+        if other == 0 and distance == 0:
+            own_load(array).wait()
+            to_across(array).wait_recv()
+            for d in range(chips - 1):
+                on_to_peer(array, d).start()
+            share(array, 1).start()
+        elif other == 0:
+            d = chips - distance - 1
+            to_peer(array, d).wait_recv()
+            share(array, 2 + d).start()
+            on_to_peer(array, d).wait_recv()
+            share(array, 1 + chips + d).start()
+        elif distance == 0:
+            share(array, 0).wait_recv()
+            share(array, 1).wait_recv()
+        else:
+            d = chips - distance - 1
+            share(array, 2 + d).wait_recv()
+            share(array, 1 + chips + d).wait_recv()
+
+    gains = [whole(4), whole(5), whole(6), whole(7)]
+    inward_bias = jnp.concatenate(
+        [
+            chunk(0, i * lines + index * (cols // 128), cols // 128)
+            for i in range(3)
+        ],
+        axis=1,
+    )
+
+    def project(u):
+        rows = rows_of(u)
+        x = inputs[rows, :].astype(f32)
+        mean = jnp.mean(x, axis=-1, keepdims=True)
+        center = x - mean
+        inverse = lax.rsqrt(jnp.mean(center * center, axis=-1, keepdims=True) + EPSILON)
+        stats[rows, 0:1] = mean
+        stats[rows, 1:2] = inverse
+        normed = center * inverse
+        first = (normed * gains[0] + gains[1]).astype(half_type)
+        first_rows[rows, :] = first
+        second_rows[rows, :] = (normed * gains[2] + gains[3]).astype(half_type)
+        projected = dot(first, inward[...]) + inward_bias
+        local = pl.ds(pl.multiple_of(z * tokens, tokens), tokens)
+        for f in range(fsdp_count):
+            at = pl.ds(pl.multiple_of((group(u) * fsdp_count + f) * tokens, tokens), tokens)
+            piece_rows = projected[f * tokens : (f + 1) * tokens, :]
+            for i in range(3):
+                value = piece_rows[:, i * cols : (i + 1) * cols]
+                if i < 2:
+                    value = turn(value, local, 1.0)
+                mixed_out[at, i * cols : (i + 1) * cols] = value.astype(half_type)
+
+    def there_copy(p):
+        owner, s = (p // own_sequences, p % own_sequences)
+        source = mixed_out.at[pl.ds(pl.multiple_of(p * tokens, tokens), tokens), :]
+        target = mixed.at[s, pl.ds(pl.multiple_of(z * tokens, tokens), tokens), :]
+        return (owner, s, source, target)
+
+    def upstream(u):
+        rows = rows_of(u)
+        value = dot(grads[rows, :], outward[...], ((1,), (1,)))
+        mixed_out[rows, 3 * cols :] = value.astype(half_type)
+        for f in range(fsdp_count):
+            p = group(u) * fsdp_count + f
+            owner, s, source, target = there_copy(p)
+
+            @pl.when(owner == z)
+            def _():
+                pltpu.make_async_copy(source, target, there_own.at[s]).start()
+
+            @pl.when(owner != z)
+            def _():
+                remote(
+                    source, target, there_sends.at[p], there_recvs.at[s, z], (b, owner, y)
+                ).start()
+
+    def there(s):
+        block_at = mixed.at[s, pl.ds(0, tokens), :]
+        pltpu.make_async_copy(block_at, block_at, there_own.at[s]).wait()
+        for d in range(1, context_count):
+            source = (z + d) % context_count
+            at = mixed.at[s, pl.ds(pl.multiple_of(source * tokens, tokens), tokens), :]
+            remote(at, at, there_sends.at[0], there_recvs.at[s, source], others[0]).wait_recv()
+
+    order = [u for u in range(0, batch_count, CORES)] + [u for u in range(1, batch_count, CORES)]
+    for array in range(2):
+        for u in order:
+            bring(array, u)
+            if array == 0:
+                if u == 0:
+                    for i in range(3):
+                        weight_loads[i].wait()
+                        weight_sends[i].wait_recv()
+                project(u)
+            else:
+                if u == 0:
+                    row_loads[0].wait()
+                upstream(u)
+
+
+    row_loads[1].wait()
+    weight_loads[3].wait()
+    weight_sends[3].wait_recv()
+    expand_bias = chunk(2, index * (unit // 128), unit // 128)
+    nothing = jnp.zeros((1, width), f32)
+
+    def normed_rows(rows):
+        return (inputs[rows, :].astype(f32) - stats[rows, 0:1]) * stats[rows, 1:2]
+
+    def forward_tile(i, carry):
+        expand_total, scale_total, shift_total = carry
+        rows = pl.ds(pl.multiple_of(i * group_rows, group_rows), group_rows)
+        before = dot(second_rows[rows, :], expand[...]) + expand_bias
+        tail = 1.0 + lax.erf(before * HALF_ROOT)
+        activated = (0.5 * before * tail).astype(half_type)
+        slope = 0.5 * tail + before * jnp.exp(-0.5 * before * before) * NORMAL_PEAK
+        before_grad = dot(grads[rows, :], contract[...], ((1,), (1,))) * slope
+        before_rows = before_grad.astype(half_type)
+        work[rows, :unit] = activated
+        work[rows, unit:] = before_rows
+        out_rows[rows, :] = dot(activated, contract[...]).astype(half_type)
+        value = dot(before_rows, expand[...], ((1,), (1,)))
+        second_back[rows, :] = value.astype(half_type)
+        return (
+            expand_total + jnp.sum(before_grad, axis=0, keepdims=True),
+            scale_total + jnp.sum(value * normed_rows(rows), axis=0, keepdims=True),
+            shift_total + jnp.sum(value, axis=0, keepdims=True),
+        )
+
+    forward_sums = lax.fori_loop(
+        0, batch_count, forward_tile, (jnp.zeros((1, unit), f32), nothing, nothing)
+    )
+
+    def expand_half(s, carry):
+        owner = (1 - y) * (1 - s) + y * s
+        column = pl.multiple_of(owner * half_width, half_width)
+        delta = dot(second_rows[:, pl.ds(column, half_width)], work[:, unit:], ((0,), (0,)))
+        group = unit * half_width // width
+        at = pl.ds(pl.multiple_of(s * group, group), group)
+        for j in range(width // unit):
+            part[at, j * unit : (j + 1) * unit] = delta[j * group : (j + 1) * group, :].astype(
+                half_type
+            )
+        return carry
+
+    lax.fori_loop(0, 2, expand_half, 0)
+    part[early_rows - unit : early_rows, :] = dot(
+        work[:, :unit], grads[...], ((0,), (0,))
+    ).astype(half_type)
 
 
     def place(half, k):
@@ -188,109 +480,149 @@
     def rows_at(ref, row):
         return ref.at[pl.ds(row, piece), :]
 
-    def final_at(slot, row):
-        return final.at[slot, pl.ds(row, piece), :]
-
-    def slot_of(k):
-        return batch_count * (1 - own(k)) + b * own(k)
-
-    def back_copy(half, k, target):
-        at = final_at(slot_of(k), place(half, k))
-        return remote(at, at, *sem(back_sems, half, k), target)
+    def sums_at(batch, row):
+        return sums_ref.at[batch, pl.ds(row, piece), :]
+
+    def back_copy(half, k, side, target):
+        at = rows_at(mine, place(half, k))
+        return remote(at, at, back_sends.at[side, half, k], back_recvs.at[half, k], target)
 
     def row_copy(half, k):
         row = place(half, k)
-        source = final_at(batch_count, row)
-        return remote(source, final_at(b, row), *sem(row_sems, half, k), across)
-
-    def chip_copy(d, half, k, slot):
-        at = final_at(slot, place(half, k))
-        return remote(at, at, *sem(chip_sems, d, half, k), peers[d])
-
-    def core_copy(d, half, k, slot):
-        at = final_at(slot, place(half, k))
-        return remote(at, at, *sem(core_sems, d, half, k), sibling)
-
-    def spread(half, k):
+        return remote(rows_at(mine, row), sums_at(b, row), *sem(row_sems, half, k), across)
+
+    def keep_copy(half, k):
+        row = place(half, k)
+        return pltpu.make_async_copy(rows_at(mine, row), sums_at(b, row), keep_sems.at[half, k])
+
+    def chip_copy(d, half, k, from_mine):
+        row = place(half, k)
+        source = rows_at(mine, row) if from_mine else sums_at(b, row)
+        return remote(source, sums_at(b, row), *sem(chip_sems, d, half, k), peers[d])
+
+    def core_copy(d, half, k, from_mine, batch):
+        row = place(half, k)
+        source = rows_at(mine, row) if from_mine else sums_at(batch, row)
+        return remote(source, sums_at(batch, row), *sem(core_sems, d, half, k), sibling)
+
+    def spread(half, k, from_mine):
         for d in range(chips - 1):
-            chip_copy(d, half, k, b).start()
-        core_copy(0, half, k, b).start()
-
-    def finish(half, k, position, behind):
-        @pl.when(position > 0)
-        def _():
-            back_copy(half, k, behind).start()
-
+            chip_copy(d, half, k, from_mine).start()
+        core_copy(0, half, k, from_mine, b).start()
+
+    def arrived(half, k):
+        for d in range(chips - 1):
+            chip_copy(d, half, k, False).wait_recv()
+            core_copy(1 + d, half, k, False, sources[d]).start()
+
+    def finish(half, k):
         @pl.when(own(k) == 0)
         def _():
             row_copy(half, k).start()
 
         @pl.when(own(k) == 1)
         def _():
-            spread(half, k)
-
-    def arrived(half, k):
-        for d in range(chips - 1):
-            chip_copy(d, half, k, sources[d]).wait_recv()
-            core_copy(1 + d, half, k, sources[d]).start()
+            keep_copy(half, k).start()
+            spread(half, k, True)
+
+    left = (b, (z + last) % context_count, y)
+    right = (b, (z + 1) % context_count, y)
+
+    def reduce_copy(half, k, source, stream, target):
+        row = place(half, k)
+        if stream:
+            landing = reduced_right.at[pl.ds(pl.multiple_of(k * piece, piece), piece), :]
+        else:
+            landing = rows_at(reduced, row)
+        return remote(
+            rows_at(source, row), landing, *sem(reduce_sems, stream, half, k), target
+        )
 
     def pieces(t, half):
-        position = z if half == 0 else last - z
-        ahead = (b, (z + 1 if half == 0 else z + last) % context_count, y)
-        behind = (b, (z + last if half == 0 else z + 1) % context_count, y)
-        k = t - position
+        root = last // 2 if half == 0 else context_count // 2
+        depth = max(root, last - root)
+        at_root = z == root
+        is_left = z < root
+        distance = jnp.where(is_left, root - z, z - root)
+        leaf = (z == 0) | (z == last)
+        k = t - LAG * (depth - distance)
+
+        def send(source):
+            @pl.when(z == root + 1)
+            def _():
+                reduce_copy(half, k, source, 1, left).start()
+
+            @pl.when(z > root + 1)
+            def _():
+                reduce_copy(half, k, source, 0, left).start()
+
+            @pl.when(is_left)
+            def _():
+                reduce_copy(half, k, source, 0, right).start()
 
         @pl.when((k >= 0) & (k < steps))
         def _():
             row = place(half, k)
-            to_next = remote(
-                rows_at(reduced, row), rows_at(reduced, row), *sem(reduce_sems, half, k), ahead
-            )
-
-            @pl.when(position == 0)
-            def _():
-                remote(
-                    rows_at(part, row), rows_at(reduced, row), *sem(reduce_sems, half, k), ahead
-                ).start()
-
-            @pl.when(position > 0)
-            def _():
-                to_next.wait_recv()
-                mine = part[pl.ds(row, piece), :].astype(f32)
-                came = reduced[pl.ds(row, piece), :].astype(f32)
-                summed = (mine + came).astype(half_type)
-
-                @pl.when(position < last)
-                def _():
-                    reduced[pl.ds(row, piece), :] = summed
-                    to_next.start()
-
-                @pl.when(position == last)
-                def _():
-                    final[slot_of(k), pl.ds(row, piece), :] = summed
-                    finish(half, k, position, behind)
-
-        k_back = t - 2 * last + position
-
-        @pl.when((position < last) & (k_back >= 0) & (k_back < steps))
+            here_at = pl.ds(row, piece)
+
+            @pl.when(at_root)
+            def _():
+                value = part[here_at, :].astype(f32)
+                if root > 0:
+                    reduce_copy(half, k, part, 0, right).wait_recv()
+                    value = value + reduced[here_at, :].astype(f32)
+                if root < last:
+                    reduce_copy(half, k, part, 1, left).wait_recv()
+                    came = reduced_right[pl.ds(pl.multiple_of(k * piece, piece), piece), :]
+                    value = value + came.astype(f32)
+                mine[here_at, :] = value.astype(half_type)
+                if root > 0:
+                    back_copy(half, k, 0, left).start()
+                if root < last:
+                    back_copy(half, k, 1, right).start()
+                finish(half, k)
+
+            @pl.when(leaf & jnp.logical_not(at_root))
+            def _():
+                send(part)
+
+            @pl.when(jnp.logical_not(leaf | at_root))
+            def _():
+                reduce_copy(half, k, part, 0, right).wait_recv()
+                value = part[here_at, :].astype(f32) + reduced[here_at, :].astype(f32)
+                reduced[here_at, :] = value.astype(half_type)
+                send(reduced)
+
+        k_back = t - LAG * (depth + distance)
+
+        @pl.when(jnp.logical_not(at_root) & (k_back >= 0) & (k_back < steps))
         def _():
-            back_copy(half, k_back, behind).wait_recv()
-            finish(half, k_back, position, behind)
-
-        k_row = k_back - 1
+            back_copy(half, k_back, 0, left).wait_recv()
+
+            @pl.when(is_left & (z > 0))
+            def _():
+                back_copy(half, k_back, 0, left).start()
+
+            @pl.when((z > root) & (z < last))
+            def _():
+                back_copy(half, k_back, 1, right).start()
+
+            finish(half, k_back)
+
+        k_row = k_back - LAG
 
         @pl.when((k_row >= 0) & (k_row < steps))
         def _():
             @pl.when(own(k_row) == 0)
             def _():
                 row_copy(half, k_row).wait_recv()
-                spread(half, k_row)
+                spread(half, k_row, False)
 
             @pl.when(own(k_row) == 1)
             def _():
                 arrived(half, k_row)
 
-        k_chip = k_row - 2
+        k_chip = k_row - 2 * LAG + 1
 
         @pl.when((k_chip >= 0) & (k_chip < steps))
         def _():
@@ -298,20 +630,56 @@
             def _():
                 arrived(half, k_chip)
 
+    def drain(k, carry):
+        for half in range(2):
+            root = last // 2 if half == 0 else context_count // 2
+            for d in range(chips):
+                core_copy(d, half, k, False, b).wait_recv()
+                core_copy(d, half, k, False, b).wait_send()
+                if d:
+                    chip_copy(d - 1, half, k, False).wait_send()
+
+            @pl.when(z == root + 1)
+            def _():
+                reduce_copy(half, k, part, 1, left).wait_send()
+
+            @pl.when((z < root) | (z > root + 1))
+            def _():
+                reduce_copy(half, k, part, 0, left).wait_send()
+
+            @pl.when((z <= root) & (z > 0))
+            def _():
+                back_copy(half, k, 0, left).wait_send()
+
+            @pl.when((z >= root) & (z < last))
+            def _():
+                back_copy(half, k, 1, right).wait_send()
+
+            @pl.when(own(k) == 0)
+            def _():
+                row_copy(half, k).wait_send()
+
+            @pl.when(own(k) == 1)
+            def _():
+                keep_copy(half, k).wait()
+
+        return carry
+
 
     def attend(n):
         s, h = (n // heads, n % heads)
         columns = [mixed[s, :, i * cols : (i + 1) * cols] for i in range(4)]
-        lane = lax.broadcasted_iota(jnp.int32, (length, cols), 1) // HEAD_DIM
-        picked = lane == h
-        nothing = jnp.zeros((length, cols), half_type)
-        queries, keys, values, upstream = columns
+        head = lax.broadcasted_iota(jnp.int32, (length, cols), 1) // HEAD_DIM
+        picked = head == h
+        blank = jnp.zeros((length, cols), half_type)
+        _, keys, values, _ = columns
         queries_h, keys_h, values_h, upstream_h = [
-            jnp.where(picked, column, nothing) for column in columns
+            jnp.where(picked, column, blank) for column in columns
         ]
         scale = 1.0 / math.sqrt(HEAD_DIM)
+        allowed = positions((1, length), 1) <= positions((length, 1), 0)
         scores = dot(queries_h, keys, ((1,), (1,))) * scale
-        scores = jnp.where(place_row[...] <= place_col[...], scores, MASKED)
+        scores = jnp.where(allowed, scores, MASKED)
         peak = jnp.max(scores, axis=1, keepdims=True)
         log_total = peak + jnp.log(jnp.sum(jnp.exp(scores - peak), axis=1, keepdims=True))
         probs = jnp.exp(scores - log_total)
@@ -344,11 +712,7 @@
             for i in range(1, 4):
                 value = heads_sum[i]
                 if i < 3:
-                    value = (
-                        value * cosine_ref[...]
-                        + pltpu.roll(value * fore_ref[...], cols - ROT // 2, 1)
-                        + pltpu.roll(value * aft_ref[...], ROT // 2, 1)
-                    )
+                    value = turn(value, slice(None), -1.0)
                 back_out[s, :, i * cols : (i + 1) * cols] = value.astype(half_type)
                 total = jnp.sum(value, axis=0, keepdims=True)
 
@@ -369,7 +733,7 @@
         row = pl.multiple_of((z * own_sequences + s) * tokens, tokens)
         destination = back_in.at[pl.ds(row, tokens), :]
         if d == 0:
-            return pltpu.make_async_copy(source, destination, own_sems.at[s])
+            return pltpu.make_async_copy(source, destination, back_own.at[s])
         return remote(source, destination, *sem(turn_sems, s, d - 1), others[d - 1])
 
     def turned():
@@ -380,23 +744,19 @@
 
 
     def head_gradients():
-        rows = first_rows.shape[0]
-        context_rows = back_in[:, :cols]
-        delta = dot(context_rows, grads[...], ((0,), (0,))).astype(half_type)
-        part[early_rows + 2 * late_other * piece * 2 :, :] = delta
-        half = width // 2
-        group = cols * half // width
-        blocks = width // cols
+        delta = dot(back_in[:, :cols], grads[...], ((0,), (0,))).astype(half_type)
+        part[early_rows + 4 * late_other * piece :, :] = delta
+        group = cols * half_width // width
 
         def half_rows(s, carry):
             owner = (1 - y) * (1 - s) + y * s
-            column = pl.multiple_of(owner * half, half)
+            column = pl.multiple_of(owner * half_width, half_width)
             delta = dot(
-                first_rows[:, pl.ds(column, half)], back_in[:, cols:], ((0,), (0,))
+                first_rows[:, pl.ds(column, half_width)], back_in[:, cols:], ((0,), (0,))
             ).astype(half_type)
             top = pl.multiple_of(early_rows + s * 3 * group, group)
             for i in range(3):
-                for j in range(blocks):
+                for j in range(width // cols):
                     part[pl.ds(top + i * group, group), j * cols : (j + 1) * cols] = delta[
                         j * group : (j + 1) * group, i * cols : (i + 1) * cols
                     ]
@@ -404,66 +764,67 @@
 
         lax.fori_loop(0, 2, half_rows, 0)
 
-    tile = min(256, plane * tokens)
-    tiles = plane * tokens // tile
-
     def output_rows():
         def step(i, carry):
-            rows = pl.ds(pl.multiple_of(i * tile, tile), tile)
+            rows = pl.ds(pl.multiple_of(i * group_rows, group_rows), group_rows)
             value = dot(back_in[rows, :cols], outward[...])
             out_rows[rows, :] = (out_rows[rows, :].astype(f32) + value).astype(half_type)
             return carry
 
-        lax.fori_loop(0, tiles, step, 0)
+        lax.fori_loop(0, batch_count, step, 0)
+
+    first_back = second_rows
+    vector_start = len(stages)
 
     def first_back_rows():
         def step(i, carry):
             scale_total, shift_total = carry
-            rows = pl.ds(pl.multiple_of(i * tile, tile), tile)
+            rows = pl.ds(pl.multiple_of(i * group_rows, group_rows), group_rows)
             value = dot(back_in[rows, cols:], inward[...], ((1,), (1,)))
             first_back[rows, :] = value.astype(half_type)
-            normed = (inputs[rows, :].astype(f32) - mean_ref[rows, :]) * inverse_ref[rows, :]
             return (
-                scale_total + jnp.sum(value * normed, axis=0, keepdims=True),
+                scale_total + jnp.sum(value * normed_rows(rows), axis=0, keepdims=True),
                 shift_total + jnp.sum(value, axis=0, keepdims=True),
             )
 
-        nothing = jnp.zeros((1, width), f32)
-        totals = lax.fori_loop(0, tiles, step, (nothing, nothing))
-        lines = width // 128
-        vector_sum[len(stages)] = vector_ref[...]
-        index = y * batch_count + b
+        first_sums = lax.fori_loop(0, batch_count, step, (nothing, nothing))
+        out = vector_sum.at[vector_start]
+        out[...] = jnp.zeros(out.shape, f32)
+
+        def put(line, value):
+            for j in range(value.shape[1] // 128):
+                out[pl.ds(line + j, 1), :] = value[:, j * 128 : (j + 1) * 128]
+
         for i in range(3):
-            for j in range(cols // 128):
-                line = i * lines + index * (cols // 128) + j
-                vector_sum[len(stages), pl.ds(line, 1), :] = inward_sum[
-                    i : i + 1, j * 128 : (j + 1) * 128
-                ]
-        first = vector_ref.shape[0] - 2 * lines
-        for i, total in enumerate(totals):
-            for j in range(lines):
-                line = first + i * lines + j
-                vector_sum[len(stages), line : line + 1, :] = total[:, j * 128 : (j + 1) * 128]
+            put(i * lines + index * (cols // 128), inward_sum[i : i + 1, :])
+        first = 3 * lines
+        own_rows = pl.ds(pl.multiple_of((b * fsdp_count + y) * tokens, tokens), tokens)
+        put(first, jnp.sum(grads[own_rows, :].astype(f32), axis=0, keepdims=True))
+        first += lines
+        put(first + index * (unit // 128), forward_sums[0])
+        first += unit * plane // 128
+        for value in forward_sums[1:] + first_sums:
+            put(first, value)
+            first += lines
 
     def vector_copy(i):
-        source = vector_sum.at[len(stages) if i == 0 else i - 1]
+        source = vector_sum.at[vector_start if i == 0 else i - 1]
         return remote(source, vector_in.at[i], *sem(vector_sems, i), stages[i])
 
 
-    arrays = (second_rows, out_rows, first_back)
-    block = fsdp_count * tokens
+    arrays = (second_back, out_rows, first_back)
 
     def near_copy(a, c):
-        row = pl.multiple_of((c * CORES + 1 - core) * block, block)
+        row = pl.multiple_of((c * CORES + 1 - core) * group_rows, group_rows)
         return remote(
-            arrays[a].at[pl.ds(row, block), :],
-            near.at[a, pl.ds(c * block, block), :],
+            arrays[a].at[pl.ds(row, group_rows), :],
+            near.at[a, pl.ds(c * group_rows, group_rows), :],
             *sem(near_sems, a, c),
             sibling,
         )
 
     def across_copy(a, c):
-        row = pl.multiple_of(c * block + (1 - y) * tokens, tokens)
+        row = pl.multiple_of(c * group_rows + (1 - y) * tokens, tokens)
         return remote(
             near.at[a, pl.ds(row, tokens), :],
             across_in.at[a, pl.ds(c * tokens, tokens), :],
@@ -486,10 +847,10 @@
             near_copy(a, c).wait_recv()
 
             def step(i, carry):
-                row = pl.multiple_of((c * CORES + core) * block + i * tokens, tokens)
-                mine = arrays[a][pl.ds(row, tokens), :].astype(f32)
-                at = pl.ds(pl.multiple_of(c * block + i * tokens, tokens), tokens)
-                near[a, at, :] = (mine + near[a, at, :].astype(f32)).astype(half_type)
+                row = pl.multiple_of((c * CORES + core) * group_rows + i * tokens, tokens)
+                value = arrays[a][pl.ds(row, tokens), :].astype(f32)
+                at = pl.ds(pl.multiple_of(c * group_rows + i * tokens, tokens), tokens)
+                near[a, at, :] = (value + near[a, at, :].astype(f32)).astype(half_type)
                 return carry
 
             lax.fori_loop(0, fsdp_count, step, 0)
@@ -500,7 +861,7 @@
             across_copy(a, c).wait_recv()
 
         def both(c):
-            row = pl.multiple_of(c * block + y * tokens, tokens)
+            row = pl.multiple_of(c * group_rows + y * tokens, tokens)
             at = pl.ds(pl.multiple_of(c * tokens, tokens), tokens)
             return (
                 near[a, pl.ds(row, tokens), :].astype(f32) + across_in[a, at, :].astype(f32),
@@ -518,7 +879,20 @@
         for d in range(chips - 1):
             far_copy(a, d).wait_recv()
             value = value + far[a, d].astype(f32)
-        token_ref[a] = value
+        own_rows = pl.ds(pl.multiple_of((b * fsdp_count + y) * tokens, tokens), tokens)
+        x = inputs[own_rows, :].astype(f32)
+        if a == 1:
+            result_ref[...] = (x + (value + whole(1)) + whole(3)).astype(half_type)
+            return
+        normed = normed_rows(own_rows)
+        scaled = value * (gains[2] if a == 0 else gains[0])
+        middle = jnp.mean(scaled, axis=-1, keepdims=True)
+        coupled = jnp.mean(scaled * normed, axis=-1, keepdims=True)
+        value = stats[own_rows, 1:2] * (scaled - middle - normed * coupled)
+        if a == 0:
+            input_grad_ref[...] = grads[own_rows, :].astype(f32) + value
+        else:
+            input_grad_ref[...] += value
 
 
     problems = own_sequences * heads
@@ -534,9 +908,9 @@
         at(slot + 6, lambda: scatter_third(a))
         at(slot + 9, lambda: scatter_last(a))
 
-    at(0, lambda: loads[2].wait())
     scatter(0, 0)
-    at(ready, lambda: [load.wait() for load in loads[3:]])
+    for s in range(own_sequences):
+        at(s * heads, lambda s=s: there(s))
     at(ready, turned)
     at(ready, head_gradients)
     at(ready + 1, output_rows)
@@ -548,66 +922,66 @@
 
         def vector_step(i=i):
             vector_copy(i).wait_recv()
-            before = vector_sum[len(stages) if i == 0 else i - 1]
+            before = vector_sum[vector_start if i == 0 else i - 1]
             vector_sum[i] = before + vector_in[i]
             if i + 1 < len(stages):
                 vector_copy(i + 1).start()
 
         at(ready + 4 + 2 * i, vector_step)
 
-    loads[0].wait()
-    loads[1].wait()
-
     def slot_step(t, carry):
         for half in range(2):
             pieces(t, half)
 
+        for slot, works in sorted(plan.items()):
+
+            @pl.when(t == slot)
+            def _():
+                for work in works:
+                    work()
+
         @pl.when(t < problems)
         def _():
             attend(t)
 
-        for slot, works in sorted(plan.items()):
-
-            @pl.when(t == slot)
-            def _():
-                for work in works:
-                    work()
-
         return carry
 
-    slots = max(steps + 2 * last + 4, max(plan) + 1)
+    depth = context_count // 2
+    tail = LAG * (2 * depth + 1)
+    slots = max(steps + tail, early + late_other + tail + 2 * LAG - 1, max(plan) + 1)
     lax.fori_loop(0, slots, slot_step, 0)
-    vector_out[...] = vector_sum[len(stages) - 1]
-
-    def drain(k, carry):
-        for half in range(2):
-            position = z if half == 0 else last - z
-            for d in range(chips):
-                core_copy(d, half, k, b).wait_recv()
-                core_copy(d, half, k, b).wait_send()
-                if d:
-                    chip_copy(d - 1, half, k, b).wait_send()
-
-            @pl.when(position < last)
-            def _():
-                row = place(half, k)
-                remote(
-                    rows_at(reduced, row), rows_at(reduced, row), *sem(reduce_sems, half, k), across
-                ).wait_send()
-
-            @pl.when(position > 0)
-            def _():
-                back_copy(half, k, across).wait_send()
-
-            @pl.when(own(k) == 0)
-            def _():
-                row_copy(half, k).wait_send()
-
-        return carry
+    first = 0
+    out_first = 0
+    for count in (3 * lines, lines, unit * plane // 128, lines, lines, lines, lines):
+        share_lines = count // fsdp_count
+        for j in range(share_lines):
+            line = first + y * share_lines + j
+            shifts_ref[out_first + j : out_first + j + 1, :] = vector_sum[
+                len(stages) - 1, pl.ds(line, 1), :
+            ]
+        first += count
+        out_first += share_lines
 
     lax.fori_loop(0, steps, drain, 0)
-    store = pltpu.make_async_copy(final.at[pl.ds(0, batch_count)], sums_ref, store_sems)
-    store.start()
+    small_copy.wait_send()
+    for send in weight_sends:
+        send.wait_send()
+    for array in range(2):
+        to_across(array).wait_send()
+        for d in range(chips - 1):
+            to_peer(array, d).wait_send()
+            on_to_peer(array, d).wait_send()
+        for i in range(2 * chips):
+            share(array, i).wait_send()
+    for p in range(plane):
+        _, _, source, target = there_copy(p)
+
+        @pl.when(p // own_sequences != z)
+        def _():
+            remote(
+                source, target, there_sends.at[p], there_recvs.at[0, 0], others[0]
+            ).wait_send()
+
     for i in range(len(stages)):
         vector_copy(i).wait_send()
     for s in range(own_sequences):
@@ -619,34 +993,17 @@
             across_copy(a, c).wait_send()
         for d in range(chips - 1):
             far_copy(a, d).wait_send()
-    store.wait()
-
-
-def back_part(
-    part,
-    mixed,
-    out_part,
-    second_part,
-    first_rows,
-    grads,
-    inputs,
-    mean,
-    inverse,
-    inward,
-    outward,
-    places,
-    tables,
-    vector,
-    tokens,
-    heads,
-    hidden,
-):
+
+
+def layer(layer_input, out_grad, span_order, small, inward, outward, expand, contract):
     sizes = tuple(lax.axis_size(name) for name in ("batch", "ctx", "fsdp"))
     batch_count, context_count, fsdp_count = sizes
     plane = batch_count * fsdp_count
     chips = batch_count // CORES
-    width = part.shape[1]
-    cols = heads * HEAD_DIM
+    tokens, width = layer_input.shape[1:]
+    hidden = expand.shape[1]
+    cols = width // plane
+    heads = cols // HEAD_DIM
     length = tokens * context_count
     own_sequences = plane // context_count
     half = width // 2
@@ -661,8 +1018,9 @@
     rows = early + late
     stage_count = (plane * context_count).bit_length() - 1
     all_tokens = plane * tokens
+    vector_lines = (8 * width + hidden) // 128
     dma = pltpu.SemaphoreType.DMA
-    f32, half_type = (jnp.float32, part.dtype)
+    f32, half_type = (jnp.float32, layer_input.dtype)
     vmem = pl.BlockSpec(memory_space=pltpu.VMEM)
     hbm = pl.BlockSpec(memory_space=pl.ANY)
 
@@ -670,82 +1028,120 @@
         return pltpu.VMEM(shape, dtype)
 
     return pl.pallas_call(
-        functools.partial(back_kernel, sizes, tokens, heads, counts, piece),
+        functools.partial(layer_kernel, sizes, tokens, heads, counts, piece),
         out_shape=(
             jax.ShapeDtypeStruct((batch_count, rows, width), half_type),
-            jax.ShapeDtypeStruct((3, tokens, width), f32),
-            jax.ShapeDtypeStruct(vector.shape, f32),
+            jax.ShapeDtypeStruct((tokens, width), half_type),
+            jax.ShapeDtypeStruct((tokens, width), f32),
+            jax.ShapeDtypeStruct((vector_lines // fsdp_count, 128), f32),
         ),
-        in_specs=[hbm] * 7 + [vmem] * 2 + [hbm] * 2 + [vmem] * 6,
-        out_specs=(hbm, vmem, vmem),
+        in_specs=[hbm, hbm, pl.BlockSpec(memory_space=pltpu.SMEM), vmem] + [hbm] * 4,
+        out_specs=(hbm, vmem, vmem, vmem),
         scratch_shapes=[
-            held(rows, width),
-            held(own_sequences, length, 4 * cols),
             held(all_tokens, width),
             held(all_tokens, width),
+            held(2, *small.shape, dtype=f32),
+            held(width, 3 * cols),
+            held(cols, width),
+            held(width, unit),
+            held(unit, width),
+            held(length, cols, dtype=f32),
+            held(length, cols, dtype=f32),
+            held(all_tokens, 2, dtype=f32),
             held(all_tokens, width),
             held(all_tokens, width),
+            held(all_tokens, 2 * unit),
             held(all_tokens, width),
             held(all_tokens, width),
-            held(width, 3 * cols),
-            held(cols, width),
-            held(8, 128),
+            held(all_tokens, 4 * cols),
+            held(own_sequences, length, 4 * cols),
             held(4, length, cols, dtype=f32),
             held(own_sequences, length, 4 * cols),
             held(all_tokens, 4 * cols),
             held(8, cols, dtype=f32),
-            held(batch_count + 1, rows, width),
             held(rows, width),
+            held(rows, width),
+            held(rows, width),
+            held(rows // 2, width),
             held(3, chips * fsdp_count * tokens, width),
             held(3, chips * tokens, width),
             held(3, chips - 1, tokens, width),
             held(3, tokens, width, dtype=f32),
-            held(stage_count, *vector.shape, dtype=f32),
-            held(stage_count + 1, *vector.shape, dtype=f32),
-            dma((9,)),
-            dma,
+            held(stage_count, vector_lines, 128, dtype=f32),
+            held(stage_count + 1, vector_lines, 128, dtype=f32),
+            dma((8,)),
+            dma((2, 1)),
+            dma((2, 4)),
+            dma((2, 2, 2 * chips - 1)),
+            dma((2, 2, 2 * chips)),
+            dma((plane,)),
+            dma((own_sequences, context_count)),
+            dma((own_sequences,)),
             dma((own_sequences,)),
             dma((2, own_sequences, context_count - 1)),
+            dma((2, 2, 2, steps)),
             dma((2, 2, steps)),
-            dma((2, 2, steps)),
+            dma((2, steps)),
             dma((2, 2, steps)),
             dma((2, chips - 1, 2, steps)),
             dma((2, chips, 2, steps)),
+            dma((2, steps)),
             dma((2, 3, chips)),
             dma((2, 3, chips)),
             dma((2, 3, chips - 1)),
             dma((2, stage_count)),
         ],
-        name="back_part",
+        name="layer",
         compiler_params=pltpu.CompilerParams(
             collective_id=0, has_side_effects=True, vmem_limit_bytes=VMEM_LIMIT
         ),
-    )(
-        part,
-        mixed,
-        out_part,
-        second_part,
-        first_rows,
-        grads,
-        inputs,
-        mean,
-        inverse,
-        inward,
-        outward,
-        *places,
-        *tables,
-        vector,
-    )
-
-
-def widen_kernel(cols, unit, turn_ref, all_ref, inward_ref, outward_ref, expand_ref, contract_ref,
-                 held, inward, outward, expand, contract, in_sems, out_sems):
+    )(layer_input, out_grad, span_order, small, inward, outward, expand, contract)
+
+
+def widen_kernel(
+    cols,
+    unit,
+    turn_ref,
+    all_ref,
+    result_in,
+    input_in,
+    shifts_in,
+    result_ref,
+    input_ref,
+    inward_ref,
+    inward_shift,
+    outward_ref,
+    outward_shift,
+    expand_ref,
+    expand_shift,
+    contract_ref,
+    contract_shift,
+    first_scale,
+    first_shift,
+    second_scale,
+    second_shift,
+    held,
+    inward,
+    outward,
+    expand,
+    contract,
+    in_sems,
+    out_sems,
+    pass_sems,
+):
     batch_count, rows, width = all_ref.shape
     half = inward_ref.shape[0]
     unit_rows, unit_blocks = (unit * half // width, width // unit)
     head_rows, head_blocks = (cols * half // width, width // cols)
     late = 2 * unit_rows + unit
     y = turn_ref[0]
+
+    handed = [
+        pltpu.make_async_copy(source, target, pass_sems.at[i])
+        for i, (source, target) in enumerate(
+            [(result_in, result_ref.at[0]), (input_in, input_ref.at[0])]
+        )
+    ]
 
     def load(b):
         return pltpu.make_async_copy(all_ref.at[b], held.at[b % 2], in_sems.at[b % 2])
@@ -787,6 +1183,22 @@
         return out
 
     load(0).start()
+    for copy in handed:
+        copy.start()
+    line = 0
+    for target in (
+        inward_shift,
+        outward_shift,
+        expand_shift,
+        second_scale,
+        second_shift,
+        first_scale,
+        first_shift,
+    ):
+        count = target.shape[0]
+        target[...] = shifts_in[line : line + count, :]
+        line += count
+    contract_shift[...] = outward_shift[...]
 
     def step(b, carry):
         at = b % 2
@@ -823,24 +1235,44 @@
     for b in range(max(0, batch_count - 2), batch_count):
         for copy in stores(b):
             copy.wait()
-
-
-def widen(gathered, cols, unit, half, hidden):
+    for copy in handed:
+        copy.wait()
+
+
+def widen(gathered, result, input_delta, shifts, cols, unit):
     batch_count, rows, width = gathered.shape
+    fsdp_count = lax.axis_size("fsdp")
+    hidden = unit * batch_count * fsdp_count
+    half = width // 2
     turn = lax.axis_index("fsdp").astype(jnp.int32)[None]
     f32 = jnp.float32
     dma = pltpu.SemaphoreType.DMA
     hbm = pl.BlockSpec(memory_space=pl.ANY)
-    return pl.pallas_call(
+    vmem = pl.BlockSpec(memory_space=pltpu.VMEM)
+
+    def matrix(rows, columns):
+        return jax.ShapeDtypeStruct((rows, columns), f32)
+
+    def vector(size):
+        return jax.ShapeDtypeStruct((size // fsdp_count // 128, 128), f32)
+
+    out = pl.pallas_call(
         functools.partial(widen_kernel, cols, unit),
         out_shape=(
-            jax.ShapeDtypeStruct((half, 3 * width), f32),
-            jax.ShapeDtypeStruct((half, width), f32),
-            jax.ShapeDtypeStruct((half, hidden), f32),
-            jax.ShapeDtypeStruct((hidden // 2, width), f32),
-        ),
-        in_specs=[pl.BlockSpec(memory_space=pltpu.SMEM), hbm],
-        out_specs=(hbm,) * 4,
+            jax.ShapeDtypeStruct((1,) + result.shape, result.dtype),
+            jax.ShapeDtypeStruct((1,) + input_delta.shape, f32),
+            matrix(half, 3 * width),
+            vector(3 * width),
+            matrix(half, width),
+            vector(width),
+            matrix(half, hidden),
+            vector(hidden),
+            matrix(hidden // 2, width),
+            vector(width),
+        )
+        + (vector(width),) * 4,
+        in_specs=[pl.BlockSpec(memory_space=pltpu.SMEM), hbm, hbm, hbm, vmem],
+        out_specs=(hbm, hbm) + (hbm, vmem) * 4 + (vmem,) * 4,
         scratch_shapes=[
             pltpu.VMEM((2, rows, width), gathered.dtype),
             pltpu.VMEM((2, 2, 3, half, cols), f32),
@@ -849,17 +1281,12 @@
             pltpu.VMEM((2, unit, width), f32),
             dma((2,)),
             dma((2, 10)),
+            dma((2,)),
         ],
         name="widen",
         compiler_params=pltpu.CompilerParams(vmem_limit_bytes=VMEM_LIMIT),
-    )(turn, gathered)
-
-
-def fold(columns, unit, half):
-    width = columns.shape[0]
-    blocks = width // unit
-    parts = columns.reshape(2, blocks, half // blocks, unit).transpose(0, 2, 1, 3)
-    return parts.reshape(2, -1, width)
+    )(turn, gathered, result, input_delta, shifts)
+    return tuple(a.reshape(-1) if a.ndim == 2 and a.shape[1] == 128 else a for a in out)
 
 
 def dot(left, right, contract=((1,), (0,))):
@@ -946,7 +1373,7 @@
     return (full.reshape(sequences, length, 4 * heads * HEAD_DIM), shift)
 
 
-def body(
+def plain_body(
     layer_input,
     out_grad,
     span_order,
@@ -1079,90 +1506,49 @@
     bias_total = jnp.sum(grad_float, axis=0)
     expand_wide = spread(expand_sum, (1, unit_cols))
 
-    if head_cols % 128 == 0:
-        slots = fold(expand_delta, unit_cols, half).astype(jnp.bfloat16)
-        slots = jnp.where(fsdp_index == 0, slots[::-1], slots).reshape(-1, width)
-        part = jnp.concatenate([slots, contract_delta.astype(jnp.bfloat16)], axis=0)
-        second_sums = [jnp.sum(second_part * normed, axis=0), jnp.sum(second_part, axis=0)]
-        nothing = jnp.zeros((width,), jnp.float32)
-        inward_wide = jnp.zeros((3 * width,), jnp.float32)
-        vectors = [inward_wide, bias_total, expand_wide, *second_sums, nothing, nothing]
-        half_rot = ROT // 2
-        blank = jnp.zeros((length, HEAD_DIM - ROT), jnp.float32)
-        zero = jnp.zeros((length, half_rot), jnp.float32)
-        tables = [
-            jnp.concatenate([cosine_all, blank + 1.0], axis=1),
-            jnp.concatenate([zero, sine_all[:, half_rot:], blank], axis=1),
-            jnp.concatenate([-sine_all[:, :half_rot], zero, blank], axis=1),
-        ]
-        tables = [jnp.tile(table, (1, heads)) for table in tables]
-        gathered, mine, whole = back_part(
-            part,
-            mixed,
-            out_part.astype(jnp.bfloat16),
-            second_part.astype(jnp.bfloat16),
-            first_rows,
-            grads_all,
-            pair_all[0],
-            jnp.mean(rows_all, axis=-1, keepdims=True),
-            inverse,
-            inward_cols,
-            outward_rows,
-            (place[:, None], place[None, :]),
-            tables,
-            jnp.concatenate(vectors).reshape(-1, 128),
-            tokens,
-            heads,
-            hidden_units,
-        )
-        totals = widen(gathered, head_cols, unit_cols, half, hidden_units)
-        whole = whole.reshape(-1)
-        order = (0, 1, 2, 5, 6, 3, 4)
-    else:
-        back, inward_sum = attention(mixed, place, cosine_all, sine_all, heads)
-        back = back.reshape(own_sequences, context_count, tokens, 4 * head_cols)
-        back = lax.all_to_all(back.transpose(1, 0, 2, 3), "ctx", 0, 0)
-        back = back.reshape(plane * tokens, 4 * head_cols)
-        context_rows = back[:, :head_cols]
-        projected_rows = back[:, head_cols:]
-        inward_delta = dot(first_rows, projected_rows, ((0,), (0,)))
-        outward_delta = dot(context_rows, grads_all, ((0,), (0,)))
-        out_part = out_part + dot(context_rows, outward_rows)
-        first_part = dot(projected_rows, inward_cols, ((1,), (1,)))
-        stacked = jnp.stack([second_part, out_part, first_part], axis=1).astype(jnp.bfloat16)
-        mine = lax.psum_scatter(stacked, PLANE, scatter_dimension=0, tiled=True)
-        mine = mine.transpose(1, 0, 2).astype(jnp.float32)
-        columns = jnp.concatenate([inward_delta, expand_delta], axis=1).astype(jnp.bfloat16)
-        rows = jnp.concatenate([outward_delta, contract_delta], axis=0).astype(jnp.bfloat16)
-        columns, rows = lax.psum((columns, rows), "ctx")
-        columns = lax.all_to_all(columns.reshape(fsdp_count, half, -1), "fsdp", 0, 0)
-        columns = lax.all_gather(columns, "batch")
-        rows = lax.all_gather(rows, "batch").astype(jnp.float32)
-        columns = columns.transpose(2, 1, 0, 3).astype(jnp.float32)
-        inward_total = columns[..., : 3 * head_cols].reshape(
-            half, fsdp_count, batch_count, 3, head_cols
-        )
-        totals = (
-            inward_total.transpose(0, 3, 1, 2, 4).reshape(half, 3 * width),
-            rows[:, :head_cols].reshape(half, width),
-            columns[..., 3 * head_cols :].reshape(half, hidden_units),
-            rows[:, head_cols:].reshape(-1, width),
-        )
-        _, second_scale, second_shift = norm_backward(
-            mine[0], normed_mine, inverse_mine, gain_second
-        )
-        _, first_scale, first_shift = norm_backward(mine[2], normed_mine, inverse_mine, gain_first)
-        vectors = [
-            spread(inward_sum, (3, head_cols)),
-            bias_total,
-            expand_wide,
-            first_scale,
-            first_shift,
-            second_scale,
-            second_shift,
-        ]
-        whole = lax.psum(jnp.concatenate(vectors), ("batch", "ctx", "fsdp"))
-        order = tuple(range(7))
+    back, inward_sum = attention(mixed, place, cosine_all, sine_all, heads)
+    back = back.reshape(own_sequences, context_count, tokens, 4 * head_cols)
+    back = lax.all_to_all(back.transpose(1, 0, 2, 3), "ctx", 0, 0)
+    back = back.reshape(plane * tokens, 4 * head_cols)
+    context_rows = back[:, :head_cols]
+    projected_rows = back[:, head_cols:]
+    inward_delta = dot(first_rows, projected_rows, ((0,), (0,)))
+    outward_delta = dot(context_rows, grads_all, ((0,), (0,)))
+    out_part = out_part + dot(context_rows, outward_rows)
+    first_part = dot(projected_rows, inward_cols, ((1,), (1,)))
+    stacked = jnp.stack([second_part, out_part, first_part], axis=1).astype(jnp.bfloat16)
+    mine = lax.psum_scatter(stacked, PLANE, scatter_dimension=0, tiled=True)
+    mine = mine.transpose(1, 0, 2).astype(jnp.float32)
+    columns = jnp.concatenate([inward_delta, expand_delta], axis=1).astype(jnp.bfloat16)
+    rows = jnp.concatenate([outward_delta, contract_delta], axis=0).astype(jnp.bfloat16)
+    columns, rows = lax.psum((columns, rows), "ctx")
+    columns = lax.all_to_all(columns.reshape(fsdp_count, half, -1), "fsdp", 0, 0)
+    columns = lax.all_gather(columns, "batch")
+    rows = lax.all_gather(rows, "batch").astype(jnp.float32)
+    columns = columns.transpose(2, 1, 0, 3).astype(jnp.float32)
+    inward_total = columns[..., : 3 * head_cols].reshape(
+        half, fsdp_count, batch_count, 3, head_cols
+    )
+    totals = (
+        inward_total.transpose(0, 3, 1, 2, 4).reshape(half, 3 * width),
+        rows[:, :head_cols].reshape(half, width),
+        columns[..., 3 * head_cols :].reshape(half, hidden_units),
+        rows[:, head_cols:].reshape(-1, width),
+    )
+    _, second_scale, second_shift = norm_backward(
+        mine[0], normed_mine, inverse_mine, gain_second
+    )
+    _, first_scale, first_shift = norm_backward(mine[2], normed_mine, inverse_mine, gain_first)
+    vectors = [
+        spread(inward_sum, (3, head_cols)),
+        bias_total,
+        expand_wide,
+        first_scale,
+        first_shift,
+        second_scale,
+        second_shift,
+    ]
+    whole = lax.psum(jnp.concatenate(vectors), ("batch", "ctx", "fsdp"))
 
     result = (hidden + (mine[1] + outward_offset) + contract_offset).astype(jnp.bfloat16)
     second_input, _, _ = norm_backward(mine[0], normed_mine, inverse_mine, gain_second)
@@ -1173,7 +1559,6 @@
         size = vector.shape[0] // fsdp_count
         halves.append(lax.dynamic_slice_in_dim(whole, start + fsdp_index * size, size, 0))
         start += vector.shape[0]
-    halves = [halves[i] for i in order]
     return (
         result[None],
         input_delta[None],
@@ -1192,6 +1577,61 @@
     )
 
 
+def body(
+    layer_input,
+    out_grad,
+    span_order,
+    inward,
+    inward_bias,
+    outward,
+    outward_bias,
+    expand,
+    expand_bias,
+    contract,
+    contract_bias,
+    first_gain,
+    first_bias,
+    second_gain,
+    second_bias,
+):
+    plane = lax.axis_size("batch") * lax.axis_size("fsdp")
+    width = layer_input.shape[2]
+    if width // plane % 128:
+        return plain_body(
+            layer_input,
+            out_grad,
+            span_order,
+            inward,
+            inward_bias,
+            outward,
+            outward_bias,
+            expand,
+            expand_bias,
+            contract,
+            contract_bias,
+            first_gain,
+            first_bias,
+            second_gain,
+            second_bias,
+        )
+    vectors = (
+        inward_bias,
+        outward_bias,
+        expand_bias,
+        contract_bias,
+        first_gain,
+        first_bias,
+        second_gain,
+        second_bias,
+    )
+    small = jnp.concatenate(vectors).astype(jnp.float32).reshape(-1, 128)
+    small = jnp.pad(small, ((0, -small.shape[0] % 8), (0, 0)))
+    sums, result, input_delta, shifts = layer(
+        layer_input, out_grad, span_order, small, inward, outward, expand, contract
+    )
+    return widen(sums, result, input_delta, shifts, width // plane, expand.shape[1] // plane)
+
+
 def solution(mesh):
     rows = P(PLANE, "ctx", None)
     matrix, vector = (P("fsdp", None), P("fsdp"))

time: 340 us -> 224 us (0.66)
  local copies, waits for them, and re-layouts: 59.5 us -> 6.56 us
  Pallas kernels: 173 us -> 215 us
  blocking collectives: 33 us -> 0 us
  matrix products: 22.4 us -> 0 us
  other arithmetic: 18.7 us -> 0.62 us
  between operations: 14.6 us -> 0.83 us
  starting transfers between devices: 9.06 us -> 0 us
  waiting for transfers between devices: 8.13 us -> 0 us
    all_gather x1 -> x0, blocking collectives: 33 us -> none  [full_vectors(): gathered = lax.all_gather(jnp.concatenate(vectors), 'fsdp')]
    pallas_call x1, Pallas kernels: 156 us -> 189 us  [layer(): pl.pallas_call(functools.partial(layer_kernel, sizes, tokens, heads, coun...]
    dot_general x8 -> x0, matrix products: 22.4 us -> none  [dot(): lax.dot_general(left, right, (contract, ((), ())), preferred_element_type...]
    dynamic_slice x8 -> x0, local copies, waits for them, and re-layouts: 10.2 us -> none  [the longest x2 4.66 us: chunk(): mine = lax.dynamic_index_in_dim(parts, batch_index, 3, keepdims=False)]
    pallas_call x1, Pallas kernels: 17.1 us -> 26.5 us  [widen(): pl.pallas_call(functools.partial(widen_kernel, cols, unit), out_shape=(ja...]
    all_to_all x2 -> x0, starting transfers between devices: 9.02 us -> none  [the longest x1 4.73 us: body(): mixed = lax.all_to_all(mixed, 'ctx', 0, 0)]
    reshape x2 -> x0, local copies, waits for them, and re-layouts: 8.34 us -> none  [the longest x1 7.98 us: chunk(): parts = array.reshape(rows, -1, fsdp_count, batch_count, cols)]
    all_to_all x2 -> x0, waiting for transfers between devices: 8.11 us -> none  [the longest x1 8.11 us: body(): mixed = lax.all_to_all(mixed, 'ctx', 0, 0)]
  transfers between devices with their start and end apart: 3 -> 0, of which waited for: 1 -> 0; matrix products, arithmetic and copies ran while one was open for 17% -> 0% of each run, Pallas kernels for 0% -> 0%
where the time goes in v1:
time: 224 us; the launch traced here: 223 us
  Pallas kernels  215 us (96%)
  local copies, waits for them, and re-layouts  6.56 us (3%)
    pallas_call x1, Pallas kernels, layer(): pl.pallas_call(functools.partial(layer_kernel, sizes, tokens, heads, coun...  189 us
    pallas_call x1, Pallas kernels, widen(): pl.pallas_call(functools.partial(widen_kernel, cols, unit), out_shape=(ja...  26.5 us
    unnamed x7, local copies, waits for them, and re-layouts  5.87 us

profile of v1, /device:TPU:0, one launch (start us, length us, event | category | flops | bytes accessed | tf_op | source)
XLA Modules:
  0.0 223.5 jit_solution(11820405456911952970)
XLA Ops:
  0.7 0.9 dynamic-update-slice
  1.6 0.9 dynamic-update-slice.1
  2.4 0.7 constant_dynamic-update-slice_fusion.1
  3.1 0.9 dynamic-update-slice.3
  4.0 0.9 dynamic-update-slice.4
  4.8 0.9 dynamic-update-slice.5
  5.7 0.9 dynamic-update-slice.6
  6.5 0.7 constant_dynamic-update-slice_fusion
  7.2 0.6 pad_convert_fusion.small_ref
  7.8 189.0 %layer.1 = (bf16[4,1536,1024]{2,1,0:T(8,128)(2,1)}, bf16[128,1024]{1,0:T(8,128)(2,1)}, f32[128,1024]{1,0:T(8,128)}, f32[48,128]{1,0:T(8,128)}) custom-call(bf16[1,128,1024]{2,1,0:T(8,128)(2,1)} %input_ref.1, bf16[1,128,1024]{2,1,0:T(8,128)(2,1)} %grad_ref.1, s32[4]{0:T(128)} %order_ref.1, f32[56,128]{1,0:T(8,128)} %pad_convert_fusion.small_ref, ...), custom_call_target="tpu_custom_call" | custom-call | tf_op jit(solution)/shard_map/layer/pallas_call | solution.py:1030
  196.8 26.5 %widen.1 = (bf16[1,128,1024]{2,1,0:T(8,128)(2,1)}, f32[1,128,1024]{2,1,0:T(8,128)}, f32[512,3072]{1,0:T(8,128)}, f32[12,128]{1,0:T(8,128)}, f32[512,1024]{1,0:T(...) custom-call(s32[1]{0:T(128)} %bitcast.turn_ref, ...), custom_call_target="tpu_custom_call" | custom-call | tf_op jit(solution)/shard_map/widen/pallas_call | solution.py:1259
  (1 shorter events, 0.0 us)

commit v2 on v1

--- a/solution.py
+++ b/solution.py
@@ -85,7 +85,7 @@
     second_rows,
     work,
     out_rows,
-    second_back,
+    scaled,
     mixed_out,
     mixed,
     heads_sum,
@@ -244,15 +244,16 @@
         load.start()
     greet([sibling, across] + peers + others)
     small_copy.start()
-    for array in range(2):
+
+    def offer(array):
         to_across(array).start()
         for d in range(chips - 1):
             to_peer(array, d).start()
         share(array, 0).start()
-        if array == 0:
-            for send in weight_sends[:3]:
-                send.start()
-    weight_sends[3].start()
+
+    offer(0)
+    for send in weight_sends[:3]:
+        send.start()
     small[0] = small_ref[...]
 
 
@@ -316,6 +317,10 @@
             for d in range(chips - 1):
                 on_to_peer(array, d).start()
             share(array, 1).start()
+            if array == 0:
+                offer(1)
+            else:
+                weight_sends[3].start()
         elif other == 0:
             d = chips - distance - 1
             to_peer(array, d).wait_recv()
@@ -432,7 +437,7 @@
         work[rows, unit:] = before_rows
         out_rows[rows, :] = dot(activated, contract[...]).astype(half_type)
         value = dot(before_rows, expand[...], ((1,), (1,)))
-        second_back[rows, :] = value.astype(half_type)
+        scaled[rows, :] = (value * gains[2]).astype(half_type)
         return (
             expand_total + jnp.sum(before_grad, axis=0, keepdims=True),
             scale_total + jnp.sum(value * normed_rows(rows), axis=0, keepdims=True),
@@ -773,7 +778,6 @@
 
         lax.fori_loop(0, batch_count, step, 0)
 
-    first_back = second_rows
     vector_start = len(stages)
 
     def first_back_rows():
@@ -781,7 +785,7 @@
             scale_total, shift_total = carry
             rows = pl.ds(pl.multiple_of(i * group_rows, group_rows), group_rows)
             value = dot(back_in[rows, cols:], inward[...], ((1,), (1,)))
-            first_back[rows, :] = value.astype(half_type)
+            scaled[rows, :] = (scaled[rows, :].astype(f32) + value * gains[0]).astype(half_type)
             return (
                 scale_total + jnp.sum(value * normed_rows(rows), axis=0, keepdims=True),
                 shift_total + jnp.sum(value, axis=0, keepdims=True),
@@ -812,7 +816,7 @@
         return remote(source, vector_in.at[i], *sem(vector_sems, i), stages[i])
 
 
-    arrays = (second_back, out_rows, first_back)
+    arrays = (out_rows, scaled)
 
     def near_copy(a, c):
         row = pl.multiple_of((c * CORES + 1 - core) * group_rows, group_rows)
@@ -881,18 +885,14 @@
             value = value + far[a, d].astype(f32)
         own_rows = pl.ds(pl.multiple_of((b * fsdp_count + y) * tokens, tokens), tokens)
         x = inputs[own_rows, :].astype(f32)
-        if a == 1:
+        if a == 0:
             result_ref[...] = (x + (value + whole(1)) + whole(3)).astype(half_type)
             return
         normed = normed_rows(own_rows)
-        scaled = value * (gains[2] if a == 0 else gains[0])
-        middle = jnp.mean(scaled, axis=-1, keepdims=True)
-        coupled = jnp.mean(scaled * normed, axis=-1, keepdims=True)
-        value = stats[own_rows, 1:2] * (scaled - middle - normed * coupled)
-        if a == 0:
-            input_grad_ref[...] = grads[own_rows, :].astype(f32) + value
-        else:
-            input_grad_ref[...] += value
+        middle = jnp.mean(value, axis=-1, keepdims=True)
+        coupled = jnp.mean(value * normed, axis=-1, keepdims=True)
+        back = stats[own_rows, 1:2] * (value - middle - normed * coupled)
+        input_grad_ref[...] = grads[own_rows, :].astype(f32) + back
 
 
     problems = own_sequences * heads
@@ -908,15 +908,14 @@
         at(slot + 6, lambda: scatter_third(a))
         at(slot + 9, lambda: scatter_last(a))
 
-    scatter(0, 0)
     for s in range(own_sequences):
         at(s * heads, lambda s=s: there(s))
     at(ready, turned)
     at(ready, head_gradients)
     at(ready + 1, output_rows)
-    scatter(1, ready + 1)
+    scatter(0, ready + 1)
     at(ready + 2, first_back_rows)
-    scatter(2, ready + 2)
+    scatter(1, ready + 2)
     at(ready + 2, lambda: vector_copy(0).start())
     for i in range(len(stages)):
 
@@ -987,7 +986,7 @@
     for s in range(own_sequences):
         for d in range(1, context_count):
             turn_copy(s, d).wait_send()
-    for a in range(3):
+    for a in range(2):
         for c in range(chips):
             near_copy(a, c).wait_send()
             across_copy(a, c).wait_send()
@@ -1063,10 +1062,10 @@
             held(rows, width),
             held(rows, width),
             held(rows // 2, width),
-            held(3, chips * fsdp_count * tokens, width),
-            held(3, chips * tokens, width),
-            held(3, chips - 1, tokens, width),
-            held(3, tokens, width, dtype=f32),
+            held(2, chips * fsdp_count * tokens, width),
+            held(2, chips * tokens, width),
+            held(2, chips - 1, tokens, width),
+            held(2, tokens, width, dtype=f32),
             held(stage_count, vector_lines, 128, dtype=f32),
             held(stage_count + 1, vector_lines, 128, dtype=f32),
             dma((8,)),
@@ -1086,9 +1085,9 @@
             dma((2, chips - 1, 2, steps)),
             dma((2, chips, 2, steps)),
             dma((2, steps)),
-            dma((2, 3, chips)),
-            dma((2, 3, chips)),
-            dma((2, 3, chips - 1)),
+            dma((2, 2, chips)),
+            dma((2, 2, chips)),
+            dma((2, 2, chips - 1)),
             dma((2, stage_count)),
         ],
         name="layer",
@@ -1127,64 +1126,47 @@
     contract,
     in_sems,
     out_sems,
-    pass_sems,
 ):
     batch_count, rows, width = all_ref.shape
     half = inward_ref.shape[0]
     unit_rows, unit_blocks = (unit * half // width, width // unit)
     head_rows, head_blocks = (cols * half // width, width // cols)
     late = 2 * unit_rows + unit
+    bounds = ((late, rows - late), (0, unit_rows), (unit_rows, unit_rows), (late - unit, unit))
     y = turn_ref[0]
 
-    handed = [
-        pltpu.make_async_copy(source, target, pass_sems.at[i])
-        for i, (source, target) in enumerate(
-            [(result_in, result_ref.at[0]), (input_in, input_ref.at[0])]
+    def load(b, part):
+        first, count = bounds[part]
+        at = pl.ds(first, count)
+        return pltpu.make_async_copy(
+            all_ref.at[b, at, :], held.at[b % 2, at, :], in_sems.at[b % 2, part]
         )
-    ]
-
-    def load(b):
-        return pltpu.make_async_copy(all_ref.at[b], held.at[b % 2], in_sems.at[b % 2])
-
-    def stores(b):
+
+    def stores(b, part):
         at = b % 2
-        sems = iter(range(2 + 2 * 4))
-        out = [
-            pltpu.make_async_copy(
-                outward.at[at],
-                outward_ref.at[pl.ds(b * cols, cols), :],
-                out_sems.at[at, next(sems)],
-            ),
-            pltpu.make_async_copy(
-                contract.at[at],
-                contract_ref.at[pl.ds(b * unit, unit), :],
-                out_sems.at[at, next(sems)],
-            ),
+        pairs = []
+        if part == 0:
+            pairs.append((outward.at[at], outward_ref.at[pl.ds(b * cols, cols), :]))
+            for s in range(2):
+                owner = y if s else 1 - y
+                for i in range(3):
+                    column = pl.multiple_of(i * width + (owner * batch_count + b) * cols, cols)
+                    pairs.append((inward.at[at, s, i], inward_ref.at[:, pl.ds(column, cols)]))
+        elif part < 3:
+            owner = y if part == 2 else 1 - y
+            column = pl.multiple_of((owner * batch_count + b) * unit, unit)
+            pairs.append((expand.at[at, part - 1], expand_ref.at[:, pl.ds(column, unit)]))
+        else:
+            pairs.append((contract.at[at], contract_ref.at[pl.ds(b * unit, unit), :]))
+        return [
+            pltpu.make_async_copy(source, target, out_sems.at[at, part, i])
+            for i, (source, target) in enumerate(pairs)
         ]
-        for s in range(2):
-            owner = y if s else 1 - y
-            column = pl.multiple_of((owner * batch_count + b) * unit, unit)
-            out.append(
-                pltpu.make_async_copy(
-                    expand.at[at, s],
-                    expand_ref.at[:, pl.ds(column, unit)],
-                    out_sems.at[at, next(sems)],
-                )
-            )
-            for i in range(3):
-                column = pl.multiple_of(i * width + (owner * batch_count + b) * cols, cols)
-                out.append(
-                    pltpu.make_async_copy(
-                        inward.at[at, s, i],
-                        inward_ref.at[:, pl.ds(column, cols)],
-                        out_sems.at[at, next(sems)],
-                    )
-                )
-        return out
-
-    load(0).start()
-    for copy in handed:
-        copy.start()
+
+    for part in range(4):
+        load(0, part).start()
+    result_ref[0] = result_in[...]
+    input_ref[0] = input_in[...]
     line = 0
     for target in (
         inward_shift,
@@ -1202,41 +1184,44 @@
 
     def step(b, carry):
         at = b % 2
-        load(b).wait()
-
-        @pl.when(b + 1 < batch_count)
-        def _():
-            load(b + 1).start()
-
-        @pl.when(b >= 2)
-        def _():
-            for copy in stores(b - 2):
-                copy.wait()
-
-        for s in range(2):
-            first = s * unit_rows
-            for i in range(unit_blocks):
-                expand[at, s, i * unit_rows : (i + 1) * unit_rows, :] = held[
-                    at, first : first + unit_rows, i * unit : (i + 1) * unit
-                ].astype(jnp.float32)
-            for part in range(3):
-                top = late + (s * 3 + part) * head_rows
-                for i in range(head_blocks):
-                    inward[at, s, part, i * head_rows : (i + 1) * head_rows, :] = held[
-                        at, top : top + head_rows, i * cols : (i + 1) * cols
+        for part in range(4):
+            load(b, part).wait()
+
+            @pl.when(b + 1 < batch_count)
+            def _():
+                load(b + 1, part).start()
+
+            @pl.when(b >= 2)
+            def _():
+                for copy in stores(b - 2, part):
+                    copy.wait()
+
+            if part == 0:
+                for s in range(2):
+                    for i in range(3):
+                        top = late + (s * 3 + i) * head_rows
+                        for j in range(head_blocks):
+                            inward[at, s, i, j * head_rows : (j + 1) * head_rows, :] = held[
+                                at, top : top + head_rows, j * cols : (j + 1) * cols
+                            ].astype(jnp.float32)
+                outward[at] = held[at, late + 6 * head_rows :, :].astype(jnp.float32)
+            elif part < 3:
+                first = (part - 1) * unit_rows
+                for j in range(unit_blocks):
+                    expand[at, part - 1, j * unit_rows : (j + 1) * unit_rows, :] = held[
+                        at, first : first + unit_rows, j * unit : (j + 1) * unit
                     ].astype(jnp.float32)
-        contract[at] = held[at, 2 * unit_rows : late, :].astype(jnp.float32)
-        outward[at] = held[at, late + 6 * head_rows :, :].astype(jnp.float32)
-        for copy in stores(b):
-            copy.start()
+            else:
+                contract[at] = held[at, late - unit : late, :].astype(jnp.float32)
+            for copy in stores(b, part):
+                copy.start()
         return carry
 
     lax.fori_loop(0, batch_count, step, 0)
     for b in range(max(0, batch_count - 2), batch_count):
-        for copy in stores(b):
-            copy.wait()
-    for copy in handed:
-        copy.wait()
+        for part in range(4):
+            for copy in stores(b, part):
+                copy.wait()
 
 
 def widen(gathered, result, input_delta, shifts, cols, unit):
@@ -1271,17 +1256,16 @@
             vector(width),
         )
         + (vector(width),) * 4,
-        in_specs=[pl.BlockSpec(memory_space=pltpu.SMEM), hbm, hbm, hbm, vmem],
-        out_specs=(hbm, hbm) + (hbm, vmem) * 4 + (vmem,) * 4,
+        in_specs=[pl.BlockSpec(memory_space=pltpu.SMEM), hbm, vmem, vmem, vmem],
+        out_specs=(vmem, vmem) + (hbm, vmem) * 4 + (vmem,) * 4,
         scratch_shapes=[
             pltpu.VMEM((2, rows, width), gathered.dtype),
             pltpu.VMEM((2, 2, 3, half, cols), f32),
             pltpu.VMEM((2, cols, width), f32),
             pltpu.VMEM((2, 2, half, unit), f32),
             pltpu.VMEM((2, unit, width), f32),
-            dma((2,)),
-            dma((2, 10)),
-            dma((2,)),
+            dma((2, 4)),
+            dma((2, 4, 7)),
         ],
         name="widen",
         compiler_params=pltpu.CompilerParams(vmem_limit_bytes=VMEM_LIMIT),
@@ -1624,8 +1608,12 @@
         second_gain,
         second_bias,
     )
-    small = jnp.concatenate(vectors).astype(jnp.float32).reshape(-1, 128)
-    small = jnp.pad(small, ((0, -small.shape[0] % 8), (0, 0)))
+    ends = [sum(v.shape[0] for v in vectors[: i + 1]) for i in range(len(vectors))]
+    room = ends[-1] + -ends[-1] % 1024
+    small = sum(
+        jnp.pad(v.astype(jnp.float32), (end - v.shape[0], room - end))
+        for v, end in zip(vectors, ends)
+    ).reshape(-1, 128)
     sums, result, input_delta, shifts = layer(
         layer_input, out_grad, span_order, small, inward, outward, expand, contract
     )

time: 224 us -> 202 us (0.902)
  Pallas kernels: 215 us -> 199 us
  local copies, waits for them, and re-layouts: 6.56 us -> 0 us
    pallas_call x1, Pallas kernels: 26.5 us -> 15.7 us  [widen(): pl.pallas_call(functools.partial(widen_kernel, cols, unit), out_shape=(ja...]
    unnamed x7 -> x0, local copies, waits for them, and re-layouts: 5.87 us -> none
    pallas_call x1, Pallas kernels: 189 us -> 184 us  [layer(): pl.pallas_call(functools.partial(layer_kernel, sizes, tokens, heads, coun...]
where the time goes in v2:
time: 202 us; the launch traced here: 201 us
  Pallas kernels  199 us (99%)
    pallas_call x1, Pallas kernels, layer(): pl.pallas_call(functools.partial(layer_kernel, sizes, tokens, heads, coun...  184 us
    pallas_call x1, Pallas kernels, widen(): pl.pallas_call(functools.partial(widen_kernel, cols, unit), out_shape=(ja...  15.7 us

profile of v2, /device:TPU:0, one launch (start us, length us, event | category | flops | bytes accessed | tf_op | source)
XLA Modules:
  0.0 201.5 jit_solution(17179021363955496430)
XLA Ops:
  0.7 1.4 add_bitcast_fusion.small_ref
  2.1 183.5 %layer.1 = (bf16[4,1536,1024]{2,1,0:T(8,128)(2,1)}, bf16[128,1024]{1,0:T(8,128)(2,1)}, f32[128,1024]{1,0:T(8,128)}, f32[48,128]{1,0:T(8,128)}) custom-call(bf16[1,128,1024]{2,1,0:T(8,128)(2,1)} %input_ref.1, bf16[1,128,1024]{2,1,0:T(8,128)(2,1)} %grad_ref.1, s32[4]{0:T(128)} %order_ref.1, f32[56,128]{1,0:T(8,128)} %add_bitcast_fusion.small_ref, ...), custom_call_target="tpu_custom_call" | custom-call | tf_op jit(solution)/shard_map/layer/pallas_call | solution.py:1029
  185.6 15.7 %widen.1 = (bf16[1,128,1024]{2,1,0:T(8,128)(2,1)}, f32[1,128,1024]{2,1,0:T(8,128)}, f32[512,3072]{1,0:T(8,128)}, f32[12,128]{1,0:T(8,128)}, f32[512,1024]{1,0:T(...) custom-call(s32[1]{0:T(128)} %bitcast.turn_ref, ...), custom_call_target="tpu_custom_call" | custom-call | tf_op jit(solution)/shard_map/widen/pallas_call | solution.py:1244

commit v3 on v2

--- a/solution.py
+++ b/solution.py
@@ -51,6 +51,12 @@
 
 
 LAG = 2
+LB = 2
+LX = 2
+LY = 3
+AHEAD = 2
+ATT = 4
+READY = 11
 
 
 def layer_kernel(
@@ -84,6 +90,8 @@
     first_rows,
     second_rows,
     work,
+    before,
+    hidden_back,
     out_rows,
     scaled,
     mixed_out,
@@ -92,6 +100,7 @@
     back_out,
     back_in,
     inward_sum,
+    row_sums,
     part,
     mine,
     reduced,
@@ -105,6 +114,7 @@
     load_sems,
     small_sems,
     weight_sems,
+    pair_sems,
     gather_sems,
     share_sems,
     there_sends,
@@ -112,13 +122,17 @@
     there_own,
     back_own,
     turn_sems,
-    reduce_sems,
+    reduce_sends,
+    reduce_recvs,
+    right_recvs,
     back_sends,
     back_recvs,
-    row_sems,
-    chip_sems,
+    row_sends,
+    row_recvs,
+    chip_sends,
+    chip_recvs,
     core_sems,
-    keep_sems,
+    keep_sem,
     near_sems,
     across_sems,
     far_sems,
@@ -203,24 +217,61 @@
             at = block(array, sources[d], y if i - 2 < chips - 1 else 1 - y)
         return remote(at, at, *sem(share_sems, array, i), sibling)
 
-    def weight_copies(owner, local):
+    def columns_of(owner, i):
+        place = owner * batch_count + b
+        if i < 3:
+            return pl.ds(pl.multiple_of(i * width + place * cols, cols), cols)
+        return pl.ds(pl.multiple_of(place * unit, unit), unit)
+
+    part_rows = half_width // 2
+    parity = z % 2
+    pair = (b, swapped(z, 1), y)
+
+    def inward_part(owner, parity):
+        first = pl.multiple_of(owner * half_width + parity * part_rows, part_rows)
+        return inward.at[pl.ds(first, part_rows), :]
+
+    def weight_copies():
+        source_rows = pl.ds(pl.multiple_of(parity * part_rows, part_rows), part_rows)
         rows = pl.ds(pl.multiple_of(y * half_width, half_width), half_width)
-        place = owner * batch_count + b
-        out = []
-        for i in range(4):
-            if i < 3:
-                column = pl.multiple_of(i * width + place * cols, cols)
-                source = inward_ref.at[:, pl.ds(column, cols)]
-                target = inward.at[rows, i * cols : (i + 1) * cols]
-            else:
-                column = pl.multiple_of(place * unit, unit)
-                source = expand_ref.at[:, pl.ds(column, unit)]
-                target = expand.at[rows, :]
-            if local:
-                out.append(pltpu.make_async_copy(source, target, load_sems.at[2 + i]))
-            else:
-                out.append(remote(source, target, *sem(weight_sems, i), across))
+        out = [
+            remote(
+                inward_ref.at[source_rows, columns_of(1 - y, i)],
+                inward_part(y, parity).at[:, i * cols : (i + 1) * cols],
+                *sem(weight_sems, 0),
+                across,
+            )
+            for i in range(3)
+        ]
+        out.append(
+            remote(
+                expand_ref.at[:, columns_of(1 - y, 3)],
+                expand.at[rows, :],
+                *sem(weight_sems, 1),
+                across,
+            )
+        )
         return out
+
+    def weight_own():
+        rows = pl.ds(pl.multiple_of(y * half_width, half_width), half_width)
+        pairs = [
+            (inward_ref.at[:, columns_of(y, i)], inward.at[rows, i * cols : (i + 1) * cols])
+            for i in range(3)
+        ]
+        pairs.append((expand_ref.at[:, columns_of(y, 3)], expand.at[rows, :]))
+        return [
+            pltpu.make_async_copy(source, target, load_sems.at[2 + i])
+            for i, (source, target) in enumerate(pairs)
+        ]
+
+    def inward_brought():
+        at = inward_part(1 - y, parity)
+        return remote(at, at, *sem(weight_sems, 0), across)
+
+    def to_pair(parity):
+        at = inward_part(1 - y, parity)
+        return remote(at, at, *sem(pair_sems), pair)
 
     row_loads = [
         pltpu.make_async_copy(
@@ -234,8 +285,8 @@
             load_sems.at[7],
         ),
     ]
-    weight_loads = weight_copies(y, True)
-    weight_sends = weight_copies(1 - y, False)
+    weight_loads = weight_own()
+    weight_sends = weight_copies()
     small_copy = remote(small_ref, small.at[1], *sem(small_sems, 0), across)
 
     own_load(0).start()
@@ -247,13 +298,16 @@
 
     def offer(array):
         to_across(array).start()
+        share(array, 0).start()
+
+    def offer_peers(array):
         for d in range(chips - 1):
             to_peer(array, d).start()
-        share(array, 0).start()
-
-    offer(0)
+
     for send in weight_sends[:3]:
         send.start()
+    offer(0)
+    offer_peers(0)
     small[0] = small_ref[...]
 
 
@@ -313,14 +367,11 @@
         distance, other = (u // CORES, u % CORES)
         if other == 0 and distance == 0:
             own_load(array).wait()
-            to_across(array).wait_recv()
+            if array == 0:
+                to_across(array).wait_recv()
             for d in range(chips - 1):
                 on_to_peer(array, d).start()
             share(array, 1).start()
-            if array == 0:
-                offer(1)
-            else:
-                weight_sends[3].start()
         elif other == 0:
             d = chips - distance - 1
             to_peer(array, d).wait_recv()
@@ -344,7 +395,7 @@
         axis=1,
     )
 
-    def project(u):
+    def norm(u):
         rows = rows_of(u)
         x = inputs[rows, :].astype(f32)
         mean = jnp.mean(x, axis=-1, keepdims=True)
@@ -353,10 +404,32 @@
         stats[rows, 0:1] = mean
         stats[rows, 1:2] = inverse
         normed = center * inverse
-        first = (normed * gains[0] + gains[1]).astype(half_type)
-        first_rows[rows, :] = first
+        first_rows[rows, :] = (normed * gains[0] + gains[1]).astype(half_type)
         second_rows[rows, :] = (normed * gains[2] + gains[3]).astype(half_type)
-        projected = dot(first, inward[...]) + inward_bias
+
+    there_columns = ((0, 3 * cols), (3 * cols, cols))
+
+    def there_copy(u, f, kind):
+        p = group(u) * fsdp_count + f
+        owner, s = (p // own_sequences, p % own_sequences)
+        first, count = there_columns[kind]
+        columns = pl.ds(first, count)
+        source = mixed_out.at[pl.ds(pl.multiple_of(p * tokens, tokens), tokens), columns]
+        at = pl.ds(pl.multiple_of(z * tokens, tokens), tokens)
+        target = mixed.at[s, at, columns]
+
+        @pl.when(owner == z)
+        def _():
+            pltpu.make_async_copy(source, target, there_own.at[s, kind]).start()
+
+        @pl.when(owner != z)
+        def _():
+            remote(
+                source, target, there_sends.at[kind], there_recvs.at[s, z, kind], (b, owner, y)
+            ).start()
+
+    def project(u):
+        projected = dot(first_rows[rows_of(u), :], inward[...]) + inward_bias
         local = pl.ds(pl.multiple_of(z * tokens, tokens), tokens)
         for f in range(fsdp_count):
             at = pl.ds(pl.multiple_of((group(u) * fsdp_count + f) * tokens, tokens), tokens)
@@ -366,89 +439,96 @@
                 if i < 2:
                     value = turn(value, local, 1.0)
                 mixed_out[at, i * cols : (i + 1) * cols] = value.astype(half_type)
-
-    def there_copy(p):
-        owner, s = (p // own_sequences, p % own_sequences)
-        source = mixed_out.at[pl.ds(pl.multiple_of(p * tokens, tokens), tokens), :]
-        target = mixed.at[s, pl.ds(pl.multiple_of(z * tokens, tokens), tokens), :]
-        return (owner, s, source, target)
+            there_copy(u, f, 0)
 
     def upstream(u):
         rows = rows_of(u)
         value = dot(grads[rows, :], outward[...], ((1,), (1,)))
         mixed_out[rows, 3 * cols :] = value.astype(half_type)
         for f in range(fsdp_count):
-            p = group(u) * fsdp_count + f
-            owner, s, source, target = there_copy(p)
-
-            @pl.when(owner == z)
-            def _():
-                pltpu.make_async_copy(source, target, there_own.at[s]).start()
-
-            @pl.when(owner != z)
-            def _():
-                remote(
-                    source, target, there_sends.at[p], there_recvs.at[s, z], (b, owner, y)
-                ).start()
+            there_copy(u, f, 1)
 
     def there(s):
-        block_at = mixed.at[s, pl.ds(0, tokens), :]
-        pltpu.make_async_copy(block_at, block_at, there_own.at[s]).wait()
-        for d in range(1, context_count):
-            source = (z + d) % context_count
-            at = mixed.at[s, pl.ds(pl.multiple_of(source * tokens, tokens), tokens), :]
-            remote(at, at, there_sends.at[0], there_recvs.at[s, source], others[0]).wait_recv()
+        for kind, (first, count) in enumerate(there_columns):
+            columns = pl.ds(first, count)
+            block_at = mixed.at[s, pl.ds(0, tokens), columns]
+            pltpu.make_async_copy(block_at, block_at, there_own.at[s, kind]).wait()
+            for d in range(1, context_count):
+                source = (z + d) % context_count
+                at = mixed.at[s, pl.ds(pl.multiple_of(source * tokens, tokens), tokens), columns]
+                recv = there_recvs.at[s, source, kind]
+                remote(at, at, there_sends.at[kind], recv, others[0]).wait_recv()
 
     order = [u for u in range(0, batch_count, CORES)] + [u for u in range(1, batch_count, CORES)]
-    for array in range(2):
-        for u in order:
-            bring(array, u)
-            if array == 0:
-                if u == 0:
-                    for i in range(3):
-                        weight_loads[i].wait()
-                        weight_sends[i].wait_recv()
-                project(u)
-            else:
-                if u == 0:
-                    row_loads[0].wait()
-                upstream(u)
+    bring(0, 0)
+    offer(1)
+    inward_brought().wait_recv()
+    to_pair(parity).start()
+    norm(0)
+    for i in range(3):
+        weight_loads[i].wait()
+    to_pair(1 - parity).wait_recv()
+    project(0)
+    to_across(1).wait_recv()
+    weight_sends[3].start()
+    for u in order[1:chips]:
+        bring(0, u)
+    offer_peers(1)
+    bring(1, 0)
+    row_loads[0].wait()
+    for u in order[1:]:
+        if u % CORES:
+            bring(0, u)
+        norm(u)
+        project(u)
+    upstream(0)
+    for u in order[1:]:
+        bring(1, u)
+        upstream(u)
 
 
     row_loads[1].wait()
     weight_loads[3].wait()
-    weight_sends[3].wait_recv()
     expand_bias = chunk(2, index * (unit // 128), unit // 128)
     nothing = jnp.zeros((1, width), f32)
 
     def normed_rows(rows):
         return (inputs[rows, :].astype(f32) - stats[rows, 0:1]) * stats[rows, 1:2]
 
-    def forward_tile(i, carry):
-        expand_total, scale_total, shift_total = carry
+    own_half = pl.ds(pl.multiple_of(y * half_width, half_width), half_width)
+    other_half = pl.ds(pl.multiple_of((1 - y) * half_width, half_width), half_width)
+
+    def early_tile(i, carry):
         rows = pl.ds(pl.multiple_of(i * group_rows, group_rows), group_rows)
-        before = dot(second_rows[rows, :], expand[...]) + expand_bias
-        tail = 1.0 + lax.erf(before * HALF_ROOT)
-        activated = (0.5 * before * tail).astype(half_type)
-        slope = 0.5 * tail + before * jnp.exp(-0.5 * before * before) * NORMAL_PEAK
-        before_grad = dot(grads[rows, :], contract[...], ((1,), (1,))) * slope
-        before_rows = before_grad.astype(half_type)
-        work[rows, :unit] = activated
-        work[rows, unit:] = before_rows
-        out_rows[rows, :] = dot(activated, contract[...]).astype(half_type)
-        value = dot(before_rows, expand[...], ((1,), (1,)))
+        before[rows, :] = dot(second_rows[rows, own_half], expand[own_half, :]) + expand_bias
+        hidden_back[rows, :] = dot(grads[rows, :], contract[...], ((1,), (1,)))
+        return carry
+
+    lax.fori_loop(0, batch_count, early_tile, 0)
+    weight_sends[3].wait_recv()
+
+    def forward_tile(i, expand_total):
+        rows = pl.ds(pl.multiple_of(i * group_rows, group_rows), group_rows)
+        value = before[rows, :] + dot(second_rows[rows, other_half], expand[other_half, :])
+        tail = 1.0 + lax.erf(value * HALF_ROOT)
+        slope = 0.5 * tail + value * jnp.exp(-0.5 * value * value) * NORMAL_PEAK
+        before_grad = hidden_back[rows, :] * slope
+        work[rows, :unit] = (0.5 * value * tail).astype(half_type)
+        work[rows, unit:] = before_grad.astype(half_type)
+        return expand_total + jnp.sum(before_grad, axis=0, keepdims=True)
+
+    expand_total = lax.fori_loop(0, batch_count, forward_tile, jnp.zeros((1, unit), f32))
+    row_sums[...] = jnp.zeros(row_sums.shape, f32)
+
+    def hidden_tile(i):
+        rows = pl.ds(pl.multiple_of(i * group_rows, group_rows), group_rows)
+        out_rows[rows, :] = dot(work[rows, :unit], contract[...]).astype(half_type)
+        value = dot(work[rows, unit:], expand[...], ((1,), (1,)))
         scaled[rows, :] = (value * gains[2]).astype(half_type)
-        return (
-            expand_total + jnp.sum(before_grad, axis=0, keepdims=True),
-            scale_total + jnp.sum(value * normed_rows(rows), axis=0, keepdims=True),
-            shift_total + jnp.sum(value, axis=0, keepdims=True),
-        )
-
-    forward_sums = lax.fori_loop(
-        0, batch_count, forward_tile, (jnp.zeros((1, unit), f32), nothing, nothing)
-    )
-
-    def expand_half(s, carry):
+        row_sums[0:1, :] += jnp.sum(value * normed_rows(rows), axis=0, keepdims=True)
+        row_sums[1:2, :] += jnp.sum(value, axis=0, keepdims=True)
+
+    def expand_half(s):
         owner = (1 - y) * (1 - s) + y * s
         column = pl.multiple_of(owner * half_width, half_width)
         delta = dot(second_rows[:, pl.ds(column, half_width)], work[:, unit:], ((0,), (0,)))
@@ -458,12 +538,13 @@
             part[at, j * unit : (j + 1) * unit] = delta[j * group : (j + 1) * group, :].astype(
                 half_type
             )
-        return carry
-
-    lax.fori_loop(0, 2, expand_half, 0)
-    part[early_rows - unit : early_rows, :] = dot(
-        work[:, :unit], grads[...], ((0,), (0,))
-    ).astype(half_type)
+
+    def contract_rows():
+        part[early_rows - unit : early_rows, :] = dot(
+            work[:, :unit], grads[...], ((0,), (0,))
+        ).astype(half_type)
+
+    expand_half(0)
 
 
     def place(half, k):
@@ -477,6 +558,9 @@
         ) * is_own
         return pl.multiple_of((2 * early * is_late + row) * piece, piece)
 
+    def other_index(k):
+        return k - (early - early_other) * jnp.minimum(k // early, 1)
+
     def own(k):
         is_late = jnp.minimum(k // early, 1)
         other = early_other * (1 - is_late) + late_other * is_late
@@ -490,35 +574,40 @@
 
     def back_copy(half, k, side, target):
         at = rows_at(mine, place(half, k))
-        return remote(at, at, back_sends.at[side, half, k], back_recvs.at[half, k], target)
+        return remote(at, at, back_sends.at[side, half], back_recvs.at[half, k], target)
 
     def row_copy(half, k):
         row = place(half, k)
-        return remote(rows_at(mine, row), sums_at(b, row), *sem(row_sems, half, k), across)
+        recv = row_recvs.at[half, other_index(k)]
+        return remote(rows_at(mine, row), sums_at(b, row), row_sends, recv, across)
 
     def keep_copy(half, k):
         row = place(half, k)
-        return pltpu.make_async_copy(rows_at(mine, row), sums_at(b, row), keep_sems.at[half, k])
+        return pltpu.make_async_copy(rows_at(mine, row), sums_at(b, row), keep_sem)
 
     def chip_copy(d, half, k, from_mine):
         row = place(half, k)
         source = rows_at(mine, row) if from_mine else sums_at(b, row)
-        return remote(source, sums_at(b, row), *sem(chip_sems, d, half, k), peers[d])
-
-    def core_copy(d, half, k, from_mine, batch):
+        return remote(
+            source, sums_at(b, row), chip_sends.at[d], chip_recvs.at[d, half, k], peers[d]
+        )
+
+    def core_copy(half, k, from_mine, batch):
         row = place(half, k)
         source = rows_at(mine, row) if from_mine else sums_at(batch, row)
-        return remote(source, sums_at(batch, row), *sem(core_sems, d, half, k), sibling)
+        return remote(
+            source, sums_at(batch, row), core_sems.at[0], core_sems.at[1], sibling
+        )
 
     def spread(half, k, from_mine):
         for d in range(chips - 1):
             chip_copy(d, half, k, from_mine).start()
-        core_copy(0, half, k, from_mine, b).start()
+        core_copy(half, k, from_mine, b).start()
 
     def arrived(half, k):
         for d in range(chips - 1):
             chip_copy(d, half, k, False).wait_recv()
-            core_copy(1 + d, half, k, False, sources[d]).start()
+            core_copy(half, k, False, sources[d]).start()
 
     def finish(half, k):
         @pl.when(own(k) == 0)
@@ -537,35 +626,53 @@
         row = place(half, k)
         if stream:
             landing = reduced_right.at[pl.ds(pl.multiple_of(k * piece, piece), piece), :]
+            recv = right_recvs.at[k]
         else:
             landing = rows_at(reduced, row)
-        return remote(
-            rows_at(source, row), landing, *sem(reduce_sems, stream, half, k), target
-        )
-
-    def pieces(t, half):
+            recv = reduce_recvs.at[half, k]
+        return remote(rows_at(source, row), landing, reduce_sends.at[half], recv, target)
+
+    def ends(half):
         root = last // 2 if half == 0 else context_count // 2
         depth = max(root, last - root)
         at_root = z == root
         is_left = z < root
         distance = jnp.where(is_left, root - z, z - root)
         leaf = (z == 0) | (z == last)
+        return root, depth, at_root, is_left, distance, leaf
+
+    def pass_on(half, k, source):
+        root = last // 2 if half == 0 else context_count // 2
+
+        @pl.when(z == root + 1)
+        def _():
+            reduce_copy(half, k, source, 1, left).start()
+
+        @pl.when(z > root + 1)
+        def _():
+            reduce_copy(half, k, source, 0, left).start()
+
+        @pl.when(z < root)
+        def _():
+            reduce_copy(half, k, source, 0, right).start()
+
+    def leaf_send(half, k):
+        pass_on(half, k, part)
+
+    def reduce_step(t, half):
+        root, depth, at_root, is_left, distance, leaf = ends(half)
         k = t - LAG * (depth - distance)
 
         def send(source):
-            @pl.when(z == root + 1)
-            def _():
-                reduce_copy(half, k, source, 1, left).start()
-
-            @pl.when(z > root + 1)
-            def _():
-                reduce_copy(half, k, source, 0, left).start()
-
-            @pl.when(is_left)
-            def _():
-                reduce_copy(half, k, source, 0, right).start()
-
-        @pl.when((k >= 0) & (k < steps))
+            pass_on(half, k, source)
+
+        k_leaf = t + AHEAD
+
+        @pl.when(leaf & jnp.logical_not(at_root) & (k_leaf < steps))
+        def _():
+            leaf_send(half, k_leaf)
+
+        @pl.when(jnp.logical_not(leaf) & (k >= 0) & (k < steps))
         def _():
             row = place(half, k)
             here_at = pl.ds(row, piece)
@@ -587,18 +694,16 @@
                     back_copy(half, k, 1, right).start()
                 finish(half, k)
 
-            @pl.when(leaf & jnp.logical_not(at_root))
-            def _():
-                send(part)
-
-            @pl.when(jnp.logical_not(leaf | at_root))
+            @pl.when(jnp.logical_not(at_root))
             def _():
                 reduce_copy(half, k, part, 0, right).wait_recv()
                 value = part[here_at, :].astype(f32) + reduced[here_at, :].astype(f32)
                 reduced[here_at, :] = value.astype(half_type)
                 send(reduced)
 
-        k_back = t - LAG * (depth + distance)
+    def back_step(t, half):
+        root, depth, at_root, is_left, distance, leaf = ends(half)
+        k_back = t - LAG * depth - LB * distance
 
         @pl.when(jnp.logical_not(at_root) & (k_back >= 0) & (k_back < steps))
         def _():
@@ -614,7 +719,9 @@
 
             finish(half, k_back)
 
-        k_row = k_back - LAG
+    def side_step(t, half):
+        root, depth, at_root, is_left, distance, leaf = ends(half)
+        k_row = t - LAG * depth - LB * distance - LX
 
         @pl.when((k_row >= 0) & (k_row < steps))
         def _():
@@ -627,7 +734,7 @@
             def _():
                 arrived(half, k_row)
 
-        k_chip = k_row - 2 * LAG + 1
+        k_chip = k_row - LY
 
         @pl.when((k_chip >= 0) & (k_chip < steps))
         def _():
@@ -635,40 +742,37 @@
             def _():
                 arrived(half, k_chip)
 
-    def drain(k, carry):
+    def drain():
+        half_rows = pl.ds(0, steps * piece)
+        other_count = 2 * (early_other + late_other) * piece
+
+        def sent(ref, semaphore):
+            remote(ref, ref, semaphore, core_sems.at[1], sibling).wait_send()
+
+        everything = sums_ref.at[pl.ds(0, chips)]
+        from_sibling = remote(everything, everything, core_sems.at[0], core_sems.at[1], sibling)
+        from_sibling.wait_send()
+        for d in range(chips - 1):
+            sent(mine, chip_sends.at[d])
+        sent(mine.at[pl.ds(0, other_count), :], row_sends)
+        kept = mine.at[pl.ds(0, mine.shape[0] - other_count), :]
+        pltpu.make_async_copy(kept, kept, keep_sem).wait()
         for half in range(2):
             root = last // 2 if half == 0 else context_count // 2
-            for d in range(chips):
-                core_copy(d, half, k, False, b).wait_recv()
-                core_copy(d, half, k, False, b).wait_send()
-                if d:
-                    chip_copy(d - 1, half, k, False).wait_send()
-
-            @pl.when(z == root + 1)
+
+            @pl.when(z != root)
             def _():
-                reduce_copy(half, k, part, 1, left).wait_send()
-
-            @pl.when((z < root) | (z > root + 1))
-            def _():
-                reduce_copy(half, k, part, 0, left).wait_send()
+                sent(mine.at[half_rows, :], reduce_sends.at[half])
 
             @pl.when((z <= root) & (z > 0))
             def _():
-                back_copy(half, k, 0, left).wait_send()
+                sent(mine.at[half_rows, :], back_sends.at[0, half])
 
             @pl.when((z >= root) & (z < last))
             def _():
-                back_copy(half, k, 1, right).wait_send()
-
-            @pl.when(own(k) == 0)
-            def _():
-                row_copy(half, k).wait_send()
-
-            @pl.when(own(k) == 1)
-            def _():
-                keep_copy(half, k).wait()
-
-        return carry
+                sent(mine.at[half_rows, :], back_sends.at[1, half])
+
+        from_sibling.wait_recv()
 
 
     def attend(n):
@@ -782,16 +886,14 @@
 
     def first_back_rows():
         def step(i, carry):
-            scale_total, shift_total = carry
             rows = pl.ds(pl.multiple_of(i * group_rows, group_rows), group_rows)
             value = dot(back_in[rows, cols:], inward[...], ((1,), (1,)))
             scaled[rows, :] = (scaled[rows, :].astype(f32) + value * gains[0]).astype(half_type)
-            return (
-                scale_total + jnp.sum(value * normed_rows(rows), axis=0, keepdims=True),
-                shift_total + jnp.sum(value, axis=0, keepdims=True),
-            )
-
-        first_sums = lax.fori_loop(0, batch_count, step, (nothing, nothing))
+            row_sums[2:3, :] += jnp.sum(value * normed_rows(rows), axis=0, keepdims=True)
+            row_sums[3:4, :] += jnp.sum(value, axis=0, keepdims=True)
+            return carry
+
+        lax.fori_loop(0, batch_count, step, 0)
         out = vector_sum.at[vector_start]
         out[...] = jnp.zeros(out.shape, f32)
 
@@ -805,10 +907,10 @@
         own_rows = pl.ds(pl.multiple_of((b * fsdp_count + y) * tokens, tokens), tokens)
         put(first, jnp.sum(grads[own_rows, :].astype(f32), axis=0, keepdims=True))
         first += lines
-        put(first + index * (unit // 128), forward_sums[0])
+        put(first + index * (unit // 128), expand_total)
         first += unit * plane // 128
-        for value in forward_sums[1:] + first_sums:
-            put(first, value)
+        for i in range(4):
+            put(first, row_sums[i : i + 1, :])
             first += lines
 
     def vector_copy(i):
@@ -896,7 +998,9 @@
 
 
     problems = own_sequences * heads
-    ready = max(early - 4, problems)
+    ready = READY
+    if ready < ATT + problems or early <= ready + AHEAD:
+        raise ValueError("schedule")
     plan = {}
 
     def at(slot, work):
@@ -908,8 +1012,12 @@
         at(slot + 6, lambda: scatter_third(a))
         at(slot + 9, lambda: scatter_last(a))
 
+    at(0, lambda: expand_half(1))
+    at(1, contract_rows)
     for s in range(own_sequences):
-        at(s * heads, lambda s=s: there(s))
+        at(ATT + s * heads, lambda s=s: there(s))
+    for i in range(batch_count):
+        at(min(ATT + problems + i, ready), lambda i=i: hidden_tile(i))
     at(ready, turned)
     at(ready, head_gradients)
     at(ready + 1, output_rows)
@@ -929,8 +1037,9 @@
         at(ready + 4 + 2 * i, vector_step)
 
     def slot_step(t, carry):
-        for half in range(2):
-            pieces(t, half)
+        for work in (reduce_step, back_step, side_step):
+            for half in range(2):
+                work(t, half)
 
         for slot, works in sorted(plan.items()):
 
@@ -939,15 +1048,22 @@
                 for work in works:
                     work()
 
-        @pl.when(t < problems)
+        @pl.when((t >= ATT) & (t < ATT + problems))
         def _():
-            attend(t)
+            attend(t - ATT)
 
         return carry
 
+    for half in range(2):
+
+        @pl.when((z == 0) | (z == last))
+        def _():
+            for k in range(AHEAD):
+                leaf_send(half, k)
+
     depth = context_count // 2
-    tail = LAG * (2 * depth + 1)
-    slots = max(steps + tail, early + late_other + tail + 2 * LAG - 1, max(plan) + 1)
+    tail = (LAG + LB) * depth + LX
+    slots = max(steps + tail, early + late_other + tail + LY, max(plan) + 1)
     lax.fori_loop(0, slots, slot_step, 0)
     first = 0
     out_first = 0
@@ -961,10 +1077,11 @@
         first += count
         out_first += share_lines
 
-    lax.fori_loop(0, steps, drain, 0)
+    drain()
     small_copy.wait_send()
-    for send in weight_sends:
-        send.wait_send()
+    inward_brought().wait_send()
+    to_pair(parity).wait_send()
+    weight_sends[3].wait_send()
     for array in range(2):
         to_across(array).wait_send()
         for d in range(chips - 1):
@@ -972,15 +1089,10 @@
             on_to_peer(array, d).wait_send()
         for i in range(2 * chips):
             share(array, i).wait_send()
-    for p in range(plane):
-        _, _, source, target = there_copy(p)
-
-        @pl.when(p // own_sequences != z)
-        def _():
-            remote(
-                source, target, there_sends.at[p], there_recvs.at[0, 0], others[0]
-            ).wait_send()
-
+    away = (plane - own_sequences) * tokens
+    for kind, (first, count) in enumerate(there_columns):
+        at = mixed_out.at[pl.ds(0, away), pl.ds(first, count)]
+        remote(at, at, there_sends.at[kind], there_recvs.at[0, 0, kind], others[0]).wait_send()
     for i in range(len(stages)):
         vector_copy(i).wait_send()
     for s in range(own_sequences):
@@ -1050,6 +1162,8 @@
             held(all_tokens, width),
             held(all_tokens, width),
             held(all_tokens, 2 * unit),
+            held(all_tokens, unit, dtype=f32),
+            held(all_tokens, unit, dtype=f32),
             held(all_tokens, width),
             held(all_tokens, width),
             held(all_tokens, 4 * cols),
@@ -1058,6 +1172,7 @@
             held(own_sequences, length, 4 * cols),
             held(all_tokens, 4 * cols),
             held(8, cols, dtype=f32),
+            held(8, width, dtype=f32),
             held(rows, width),
             held(rows, width),
             held(rows, width),
@@ -1070,21 +1185,26 @@
             held(stage_count + 1, vector_lines, 128, dtype=f32),
             dma((8,)),
             dma((2, 1)),
-            dma((2, 4)),
+            dma((2, 2)),
+            dma((2,)),
             dma((2, 2, 2 * chips - 1)),
             dma((2, 2, 2 * chips)),
-            dma((plane,)),
-            dma((own_sequences, context_count)),
-            dma((own_sequences,)),
+            dma((2,)),
+            dma((own_sequences, context_count, 2)),
+            dma((own_sequences, 2)),
             dma((own_sequences,)),
             dma((2, own_sequences, context_count - 1)),
-            dma((2, 2, 2, steps)),
-            dma((2, 2, steps)),
+            dma((2,)),
             dma((2, steps)),
-            dma((2, 2, steps)),
-            dma((2, chips - 1, 2, steps)),
-            dma((2, chips, 2, steps)),
+            dma((steps,)),
+            dma((2, 2)),
             dma((2, steps)),
+            dma,
+            dma((2, counts[0] + counts[2])),
+            dma((chips - 1,)),
+            dma((chips - 1, 2, steps)),
+            dma((2,)),
+            dma,
             dma((2, 2, chips)),
             dma((2, 2, chips)),
             dma((2, 2, chips - 1)),
@@ -1139,7 +1259,7 @@
         first, count = bounds[part]
         at = pl.ds(first, count)
         return pltpu.make_async_copy(
-            all_ref.at[b, at, :], held.at[b % 2, at, :], in_sems.at[b % 2, part]
+            all_ref.at[b, at, :], held.at[b, at, :], in_sems.at[b, part]
         )
 
     def stores(b, part):
@@ -1163,8 +1283,9 @@
             for i, (source, target) in enumerate(pairs)
         ]
 
-    for part in range(4):
-        load(0, part).start()
+    for b in range(batch_count):
+        for part in range(4):
+            load(b, part).start()
     result_ref[0] = result_in[...]
     input_ref[0] = input_in[...]
     line = 0
@@ -1187,10 +1308,6 @@
         for part in range(4):
             load(b, part).wait()
 
-            @pl.when(b + 1 < batch_count)
-            def _():
-                load(b + 1, part).start()
-
             @pl.when(b >= 2)
             def _():
                 for copy in stores(b - 2, part):
@@ -1202,17 +1319,17 @@
                         top = late + (s * 3 + i) * head_rows
                         for j in range(head_blocks):
                             inward[at, s, i, j * head_rows : (j + 1) * head_rows, :] = held[
-                                at, top : top + head_rows, j * cols : (j + 1) * cols
+                                b, top : top + head_rows, j * cols : (j + 1) * cols
                             ].astype(jnp.float32)
-                outward[at] = held[at, late + 6 * head_rows :, :].astype(jnp.float32)
+                outward[at] = held[b, late + 6 * head_rows :, :].astype(jnp.float32)
             elif part < 3:
                 first = (part - 1) * unit_rows
                 for j in range(unit_blocks):
                     expand[at, part - 1, j * unit_rows : (j + 1) * unit_rows, :] = held[
-                        at, first : first + unit_rows, j * unit : (j + 1) * unit
+                        b, first : first + unit_rows, j * unit : (j + 1) * unit
                     ].astype(jnp.float32)
             else:
-                contract[at] = held[at, late - unit : late, :].astype(jnp.float32)
+                contract[at] = held[b, late - unit : late, :].astype(jnp.float32)
             for copy in stores(b, part):
                 copy.start()
         return carry
@@ -1259,12 +1376,12 @@
         in_specs=[pl.BlockSpec(memory_space=pltpu.SMEM), hbm, vmem, vmem, vmem],
         out_specs=(vmem, vmem) + (hbm, vmem) * 4 + (vmem,) * 4,
         scratch_shapes=[
-            pltpu.VMEM((2, rows, width), gathered.dtype),
+            pltpu.VMEM((batch_count, rows, width), gathered.dtype),
             pltpu.VMEM((2, 2, 3, half, cols), f32),
             pltpu.VMEM((2, cols, width), f32),
             pltpu.VMEM((2, 2, half, unit), f32),
             pltpu.VMEM((2, unit, width), f32),
-            dma((2, 4)),
+            dma((batch_count, 4)),
             dma((2, 4, 7)),
         ],
         name="widen",

time: 202 us -> 188 us (0.931)
  Pallas kernels: 199 us -> 185 us
    pallas_call x1, Pallas kernels: 184 us -> 171 us  [layer(): pl.pallas_call(functools.partial(layer_kernel, sizes, tokens, heads, coun...]
where the time goes in v3:
time: 188 us
  Pallas kernels  185 us (98%)
    pallas_call x1, Pallas kernels, layer(): pl.pallas_call(functools.partial(layer_kernel, sizes, tokens, heads, coun...  171 us
    pallas_call x1, Pallas kernels, widen(): pl.pallas_call(functools.partial(widen_kernel, cols, unit), out_shape=(ja...  14.6 us

profile of v3, /device:TPU:0, one launch (start us, length us, event | category | flops | bytes accessed | tf_op | source)
XLA Modules:
  0.0 187.7 jit_solution(3194287690361632237)
XLA Ops:
  0.7 1.4 add_bitcast_fusion.small_ref
  2.1 170.9 %layer.1 = (bf16[4,1536,1024]{2,1,0:T(8,128)(2,1)}, bf16[128,1024]{1,0:T(8,128)(2,1)}, f32[128,1024]{1,0:T(8,128)}, f32[48,128]{1,0:T(8,128)}) custom-call(bf16[1,128,1024]{2,1,0:T(8,128)(2,1)} %input_ref.1, bf16[1,128,1024]{2,1,0:T(8,128)(2,1)} %grad_ref.1, s32[4]{0:T(128)} %order_ref.1, f32[56,128]{1,0:T(8,128)} %add_bitcast_fusion.small_ref, ...), custom_call_target="tpu_custom_call" | custom-call | tf_op jit(solution)/shard_map/layer/pallas_call | solution.py:1141
  173.0 14.6 %widen.1 = (bf16[1,128,1024]{2,1,0:T(8,128)(2,1)}, f32[1,128,1024]{2,1,0:T(8,128)}, f32[512,3072]{1,0:T(8,128)}, f32[12,128]{1,0:T(8,128)}, f32[512,1024]{1,0:T(...) custom-call(s32[1]{0:T(128)} %bitcast.turn_ref, ...), custom_call_target="tpu_custom_call" | custom-call | tf_op jit(solution)/shard_map/widen/pallas_call | solution.py:1361

commit v4 on v3

--- a/solution.py
+++ b/solution.py
@@ -308,6 +308,9 @@
         send.start()
     offer(0)
     offer_peers(0)
+    offer(1)
+    offer_peers(1)
+    weight_sends[3].start()
     small[0] = small_ref[...]
 
 
@@ -461,7 +464,6 @@
 
     order = [u for u in range(0, batch_count, CORES)] + [u for u in range(1, batch_count, CORES)]
     bring(0, 0)
-    offer(1)
     inward_brought().wait_recv()
     to_pair(parity).start()
     norm(0)
@@ -470,10 +472,8 @@
     to_pair(1 - parity).wait_recv()
     project(0)
     to_across(1).wait_recv()
-    weight_sends[3].start()
     for u in order[1:chips]:
         bring(0, u)
-    offer_peers(1)
     bring(1, 0)
     row_loads[0].wait()
     for u in order[1:]:
@@ -1246,6 +1246,8 @@
     contract,
     in_sems,
     out_sems,
+    outward_sems,
+    wide_sems,
 ):
     batch_count, rows, width = all_ref.shape
     half = inward_ref.shape[0]
@@ -1266,12 +1268,7 @@
         at = b % 2
         pairs = []
         if part == 0:
-            pairs.append((outward.at[at], outward_ref.at[pl.ds(b * cols, cols), :]))
-            for s in range(2):
-                owner = y if s else 1 - y
-                for i in range(3):
-                    column = pl.multiple_of(i * width + (owner * batch_count + b) * cols, cols)
-                    pairs.append((inward.at[at, s, i], inward_ref.at[:, pl.ds(column, cols)]))
+            pairs.append((outward.at[b], outward_ref.at[pl.ds(b * cols, cols), :]))
         elif part < 3:
             owner = y if part == 2 else 1 - y
             column = pl.multiple_of((owner * batch_count + b) * unit, unit)
@@ -1279,12 +1276,32 @@
         else:
             pairs.append((contract.at[at], contract_ref.at[pl.ds(b * unit, unit), :]))
         return [
-            pltpu.make_async_copy(source, target, out_sems.at[at, part, i])
-            for i, (source, target) in enumerate(pairs)
+            pltpu.make_async_copy(
+                source, target, outward_sems.at[b] if part == 0 else out_sems.at[at, part - 1]
+            )
+            for source, target in pairs
         ]
 
+    def wide_stores():
+        group = batch_count * cols
+        out = []
+        for s in range(2):
+            owner = y if s else 1 - y
+            for i in range(3):
+                column = pl.multiple_of(i * width + owner * group, group)
+                out.append(
+                    pltpu.make_async_copy(
+                        inward.at[s, i],
+                        inward_ref.at[:, pl.ds(column, group)],
+                        wide_sems.at[s, i],
+                    )
+                )
+        return out
+
     for b in range(batch_count):
-        for part in range(4):
+        load(b, 0).start()
+    for b in range(batch_count):
+        for part in range(1, 4):
             load(b, part).start()
     result_ref[0] = result_in[...]
     input_ref[0] = input_in[...]
@@ -1303,9 +1320,24 @@
         line += count
     contract_shift[...] = outward_shift[...]
 
+    for b in range(batch_count):
+        load(b, 0).wait()
+        for s in range(2):
+            for i in range(3):
+                top = late + (s * 3 + i) * head_rows
+                for j in range(head_blocks):
+                    inward[
+                        s, i, j * head_rows : (j + 1) * head_rows, b * cols : (b + 1) * cols
+                    ] = held[b, top : top + head_rows, j * cols : (j + 1) * cols].astype(jnp.float32)
+        outward[b] = held[b, late + 6 * head_rows :, :].astype(jnp.float32)
+        for copy in stores(b, 0):
+            copy.start()
+    for copy in wide_stores():
+        copy.start()
+
     def step(b, carry):
         at = b % 2
-        for part in range(4):
+        for part in range(1, 4):
             load(b, part).wait()
 
             @pl.when(b >= 2)
@@ -1313,16 +1345,7 @@
                 for copy in stores(b - 2, part):
                     copy.wait()
 
-            if part == 0:
-                for s in range(2):
-                    for i in range(3):
-                        top = late + (s * 3 + i) * head_rows
-                        for j in range(head_blocks):
-                            inward[at, s, i, j * head_rows : (j + 1) * head_rows, :] = held[
-                                b, top : top + head_rows, j * cols : (j + 1) * cols
-                            ].astype(jnp.float32)
-                outward[at] = held[b, late + 6 * head_rows :, :].astype(jnp.float32)
-            elif part < 3:
+            if part < 3:
                 first = (part - 1) * unit_rows
                 for j in range(unit_blocks):
                     expand[at, part - 1, j * unit_rows : (j + 1) * unit_rows, :] = held[
@@ -1335,10 +1358,13 @@
         return carry
 
     lax.fori_loop(0, batch_count, step, 0)
-    for b in range(max(0, batch_count - 2), batch_count):
+    for b in range(batch_count):
         for part in range(4):
-            for copy in stores(b, part):
-                copy.wait()
+            if part == 0 or b >= batch_count - 2:
+                for copy in stores(b, part):
+                    copy.wait()
+    for copy in wide_stores():
+        copy.wait()
 
 
 def widen(gathered, result, input_delta, shifts, cols, unit):
@@ -1377,12 +1403,14 @@
         out_specs=(vmem, vmem) + (hbm, vmem) * 4 + (vmem,) * 4,
         scratch_shapes=[
             pltpu.VMEM((batch_count, rows, width), gathered.dtype),
-            pltpu.VMEM((2, 2, 3, half, cols), f32),
-            pltpu.VMEM((2, cols, width), f32),
+            pltpu.VMEM((2, 3, half, batch_count * cols), f32),
+            pltpu.VMEM((batch_count, cols, width), f32),
             pltpu.VMEM((2, 2, half, unit), f32),
             pltpu.VMEM((2, unit, width), f32),
             dma((batch_count, 4)),
-            dma((2, 4, 7)),
+            dma((2, 3)),
+            dma((batch_count,)),
+            dma((2, 3)),
         ],
         name="widen",
         compiler_params=pltpu.CompilerParams(vmem_limit_bytes=VMEM_LIMIT),

time: 188 us -> 182 us (0.968)
  Pallas kernels: 185 us -> 179 us
    pallas_call x1, Pallas kernels: 171 us -> 165 us  [layer(): pl.pallas_call(functools.partial(layer_kernel, sizes, tokens, heads, coun...]
where the time goes in v4:
time: 182 us; the launch traced here: 181 us
  Pallas kernels  179 us (98%)
    pallas_call x1, Pallas kernels, layer(): pl.pallas_call(functools.partial(layer_kernel, sizes, tokens, heads, coun...  165 us
    pallas_call x1, Pallas kernels, widen(): pl.pallas_call(functools.partial(widen_kernel, cols, unit), out_shape=(ja...  14.2 us

profile of v4, /device:TPU:0, one launch (start us, length us, event | category | flops | bytes accessed | tf_op | source)
XLA Modules:
  0.0 181.4 jit_solution(9757491911947226085)
XLA Ops:
  0.7 1.4 add_bitcast_fusion.small_ref
  2.1 165.0 %layer.1 = (bf16[4,1536,1024]{2,1,0:T(8,128)(2,1)}, bf16[128,1024]{1,0:T(8,128)(2,1)}, f32[128,1024]{1,0:T(8,128)}, f32[48,128]{1,0:T(8,128)}) custom-call(bf16[1,128,1024]{2,1,0:T(8,128)(2,1)} %input_ref.1, bf16[1,128,1024]{2,1,0:T(8,128)(2,1)} %grad_ref.1, s32[4]{0:T(128)} %order_ref.1, f32[56,128]{1,0:T(8,128)} %add_bitcast_fusion.small_ref, ...), custom_call_target="tpu_custom_call" | custom-call | tf_op jit(solution)/shard_map/layer/pallas_call | solution.py:1141
  167.1 14.2 %widen.1 = (bf16[1,128,1024]{2,1,0:T(8,128)(2,1)}, f32[1,128,1024]{2,1,0:T(8,128)}, f32[512,3072]{1,0:T(8,128)}, f32[12,128]{1,0:T(8,128)}, f32[512,1024]{1,0:T(...) custom-call(s32[1]{0:T(128)} %bitcast.turn_ref, ...), custom_call_target="tpu_custom_call" | custom-call | tf_op jit(solution)/shard_map/widen/pallas_call | solution.py:1387

commit v5 on v4

--- a/solution.py
+++ b/solution.py
@@ -1034,7 +1034,7 @@
             if i + 1 < len(stages):
                 vector_copy(i + 1).start()
 
-        at(ready + 4 + 2 * i, vector_step)
+        at(ready + 4 + 3 * i, vector_step)
 
     def slot_step(t, carry):
         for work in (reduce_step, back_step, side_step):

time: 182 us -> 182 us (level)
  no operation moved by 1% of the time
where the time goes in v5:
time: 182 us; the launch traced here: 181 us
  Pallas kernels  179 us (98%)
    pallas_call x1, Pallas kernels, layer(): pl.pallas_call(functools.partial(layer_kernel, sizes, tokens, heads, coun...  165 us
    pallas_call x1, Pallas kernels, widen(): pl.pallas_call(functools.partial(widen_kernel, cols, unit), out_shape=(ja...  14.2 us

profile of v5, /device:TPU:0, one launch (start us, length us, event | category | flops | bytes accessed | tf_op | source)
XLA Modules:
  0.0 181.4 jit_solution(14830938218610161056)
XLA Ops:
  0.7 1.4 add_bitcast_fusion.small_ref
  2.1 165.0 %layer.1 = (bf16[4,1536,1024]{2,1,0:T(8,128)(2,1)}, bf16[128,1024]{1,0:T(8,128)(2,1)}, f32[128,1024]{1,0:T(8,128)}, f32[48,128]{1,0:T(8,128)}) custom-call(bf16[1,128,1024]{2,1,0:T(8,128)(2,1)} %input_ref.1, bf16[1,128,1024]{2,1,0:T(8,128)(2,1)} %grad_ref.1, s32[4]{0:T(128)} %order_ref.1, f32[56,128]{1,0:T(8,128)} %add_bitcast_fusion.small_ref, ...), custom_call_target="tpu_custom_call" | custom-call | tf_op jit(solution)/shard_map/layer/pallas_call | solution.py:1141
  167.1 14.2 %widen.1 = (bf16[1,128,1024]{2,1,0:T(8,128)(2,1)}, f32[1,128,1024]{2,1,0:T(8,128)}, f32[512,3072]{1,0:T(8,128)}, f32[12,128]{1,0:T(8,128)}, f32[512,1024]{1,0:T(...) custom-call(s32[1]{0:T(128)} %bitcast.turn_ref, ...), custom_call_target="tpu_custom_call" | custom-call | tf_op jit(solution)/shard_map/widen/pallas_call | solution.py:1387

commit v6 on v5

--- a/solution.py
+++ b/solution.py
@@ -1017,7 +1017,7 @@
     for s in range(own_sequences):
         at(ATT + s * heads, lambda s=s: there(s))
     for i in range(batch_count):
-        at(min(ATT + problems + i, ready), lambda i=i: hidden_tile(i))
+        at(2 + i // 2, lambda i=i: hidden_tile(i))
     at(ready, turned)
     at(ready, head_gradients)
     at(ready + 1, output_rows)
@@ -1034,7 +1034,7 @@
             if i + 1 < len(stages):
                 vector_copy(i + 1).start()
 
-        at(ready + 4 + 3 * i, vector_step)
+        at(ready + 5 + 4 * i, vector_step)
 
     def slot_step(t, carry):
         for work in (reduce_step, back_step, side_step):

time: 182 us -> 182 us (level)
  no operation moved by 1% of the time
where the time goes in v6:
time: 182 us; the launch traced here: 181 us
  Pallas kernels  179 us (98%)
    pallas_call x1, Pallas kernels, layer(): pl.pallas_call(functools.partial(layer_kernel, sizes, tokens, heads, coun...  165 us
    pallas_call x1, Pallas kernels, widen(): pl.pallas_call(functools.partial(widen_kernel, cols, unit), out_shape=(ja...  14.2 us

profile of v6, /device:TPU:0, one launch (start us, length us, event | category | flops | bytes accessed | tf_op | source)
XLA Modules:
  0.0 181.5 jit_solution(2121967709285970520)
XLA Ops:
  0.7 1.4 add_bitcast_fusion.small_ref
  2.1 165.1 %layer.1 = (bf16[4,1536,1024]{2,1,0:T(8,128)(2,1)}, bf16[128,1024]{1,0:T(8,128)(2,1)}, f32[128,1024]{1,0:T(8,128)}, f32[48,128]{1,0:T(8,128)}) custom-call(bf16[1,128,1024]{2,1,0:T(8,128)(2,1)} %input_ref.1, bf16[1,128,1024]{2,1,0:T(8,128)(2,1)} %grad_ref.1, s32[4]{0:T(128)} %order_ref.1, f32[56,128]{1,0:T(8,128)} %add_bitcast_fusion.small_ref, ...), custom_call_target="tpu_custom_call" | custom-call | tf_op jit(solution)/shard_map/layer/pallas_call | solution.py:1141
  167.1 14.2 %widen.1 = (bf16[1,128,1024]{2,1,0:T(8,128)(2,1)}, f32[1,128,1024]{2,1,0:T(8,128)}, f32[512,3072]{1,0:T(8,128)}, f32[12,128]{1,0:T(8,128)}, f32[512,1024]{1,0:T(...) custom-call(s32[1]{0:T(128)} %bitcast.turn_ref, ...), custom_call_target="tpu_custom_call" | custom-call | tf_op jit(solution)/shard_map/widen/pallas_call | solution.py:1387
